TPU v7x, 32 devices: a whole 2x2x4 slice. The times are simulated.
32 devices in a mesh: dom: 8 (over y, x, core), grp: 4 (over z).
Axes of the slice: x: 2, y: 2, z: 4, core: 2. Of those that a mesh axis runs over, the one named last changes fastest.
Arguments:
- valence: float32 [64, 64, 512], P('dom', None, 'grp')
- start_potential: float32 [64, 64, 512], P('dom', None, 'grp'), may hold values from -3 to 3
- atom_tiles: float32 [8192, 512], P(('dom', 'grp')), may hold values from -12 to 12
- atom_home: int32 [8192, 1], P(('dom', 'grp')), may hold values from 0 to 31; in each aligned block of 256 rows (0 to 255, 256 to 511, ...) at most 16 rows name the same one
- atom_offset_x: int32 [8192, 1], P(('dom', 'grp')), may hold values from 0 to 7
- atom_offset_y: int32 [8192, 1], P(('dom', 'grp')), may hold values from 0 to 63
- atom_offset_z: int32 [8192, 1], P(('dom', 'grp')), may hold values from 0 to 120
- atom_size: int32 [8192, 1], P(('dom', 'grp')), may hold values from 4 to 8
Outputs:
- potential: float32 [64, 64, 512], P('dom', None, 'grp')
- stress: float32 [6], replicated
Inputs may be any that keep to these rules, and one draw needn't show every extreme that they name: `atom_home`: at most 16 atoms among the rows of one device share a home, and some home has exactly 16 of them.
All inputs are finite; a program needn't handle non-finite values.
Results may differ from a plain program's by a relative error of at most 0.00014.
Values sent between devices are 32-bit elements; how exact they have to be, the bound alone decides.
A program may use at most 128 MiB of HBM per device.

v0:
```python
import jax
import jax.numpy as jnp
from jax import lax
from jax.sharding import PartitionSpec as P

TE = 8
NU = 2


DAMPING = 2.0 / 3.0


def extended(value, sides, width):
    for axis, dim in sides:
        peers, length = (lax.axis_size(axis), value.shape[dim])
        up = [(i, (i + 1) % peers) for i in range(peers - 1)]
        down = [(j, i) for i, j in up]
        last = lax.slice_in_dim(value, length - width, length, axis=dim)
        leading = lax.slice_in_dim(value, 0, width, axis=dim)
        before = lax.ppermute(last, axis, up)
        after = lax.ppermute(leading, axis, down)
        value = jnp.concatenate([before, value, after], axis=dim)
    return value


def from_behind(block, axis, distance):
    devices = range(lax.axis_size(axis))
    route = [(i - distance, i) for i in devices if i - distance in devices]
    return lax.ppermute(block, axis, route)


def sine_basis(length_now):
    steps_now = jnp.arange(length_now, dtype=jnp.float32)
    table = jnp.sqrt(2.0 / (length_now + 1)) * jnp.sin(
        jnp.pi * (steps_now[:, None] + 1.0) * (steps_now[None, :] + 1.0) / (length_now + 1)
    )
    values = 2.0 - 2.0 * jnp.cos(jnp.pi * (steps_now + 1.0) / (length_now + 1))
    return (table, values)


def cyclic_basis(length_now):
    steps_now = jnp.arange(length_now, dtype=jnp.float32)[:, None]
    column = jnp.arange(length_now, dtype=jnp.int32)[None, :]
    freqs = ((column + 1) // 2).astype(jnp.float32)
    angles = 2.0 * jnp.pi * freqs * steps_now / length_now
    use_sine = (column % 2 == 0) & (column > 0)
    edge_cols = (column == 0) | (column == length_now - 1)
    scales = jnp.where(edge_cols, jnp.sqrt(1.0 / length_now), jnp.sqrt(2.0 / length_now))
    table = scales * jnp.where(use_sine, jnp.sin(angles), jnp.cos(angles))
    values = 2.0 - 2.0 * jnp.cos(2.0 * jnp.pi * freqs[0] / length_now)
    return (table, values)


def exact_solve(source, spacing_sq):
    table_x, values_x = sine_basis(source.shape[0])
    table_y, values_y = cyclic_basis(source.shape[1])
    table_z, values_z = sine_basis(source.shape[2])
    highest = lax.Precision.HIGHEST
    modes = jnp.einsum("ia,ijk->ajk", table_x, source, precision=highest)
    modes = jnp.einsum("jb,ajk->abk", table_y, modes, precision=highest)
    modes = jnp.einsum("kc,abk->abc", table_z, modes, precision=highest)
    modes = (
        modes
        * spacing_sq
        / (values_x[:, None, None] + values_y[None, :, None] + values_z[None, None, :])
    )
    result = jnp.einsum("kc,abc->abk", table_z, modes, precision=highest)
    result = jnp.einsum("jb,abk->ajk", table_y, result, precision=highest)
    return jnp.einsum("ia,ajk->ijk", table_x, result, precision=highest)


def neighbours(current, layout):
    if layout == "split":
        return extended(current, (("dom", 0), ("grp", 2)), 1)
    return jnp.pad(current, ((1, 1), (0, 0), (1, 1)))


def operate(current, spacing_sq, layout):
    padded = neighbours(current, layout)
    beside = padded[2:, :, 1:-1] + padded[:-2, :, 1:-1]
    beside = beside + jnp.roll(current, 1, axis=1) + jnp.roll(current, -1, axis=1)
    beside = beside + padded[1:-1, :, 2:] + padded[1:-1, :, :-2]
    return (6.0 * current - beside) / spacing_sq


def smooth(current, source, spacing_sq, sweeps, layout):
    for step_index in range(sweeps):
        if current is None:
            current = DAMPING * spacing_sq / 6.0 * source
        else:
            current = current + DAMPING * spacing_sq / 6.0 * (
                source - operate(current, spacing_sq, layout)
            )
    return current


def restrict(residue):
    dims_now = residue.shape
    coarse = residue.reshape(dims_now[0] // 2, 2, dims_now[1] // 2, 2, dims_now[2] // 2, 2)
    return coarse.mean(axis=(1, 3, 5))


def prolong(correction):
    dims_now = correction.shape
    spread = jnp.broadcast_to(
        correction[:, None, :, None, :, None], (dims_now[0], 2, dims_now[1], 2, dims_now[2], 2)
    )
    return spread.reshape(dims_now[0] * 2, dims_now[1] * 2, dims_now[2] * 2)


def vcycle(level_index, current, source, layout, gather_level):
    if layout == "split" and level_index == gather_level:
        column = lax.all_gather(source, "grp", axis=2, tiled=True)
        whole_grid = lax.all_gather(column, "dom", axis=0, tiled=True)
        joined = vcycle(level_index, None, whole_grid, "whole", gather_level)
        own_width = source.shape[0]
        own_depth = source.shape[2]
        mine = lax.dynamic_slice_in_dim(joined, lax.axis_index("dom") * own_width, own_width, 0)
        return lax.dynamic_slice_in_dim(mine, lax.axis_index("grp") * own_depth, own_depth, 2)
    spacing_sq = 4.0**level_index
    if level_index == 3:
        return exact_solve(source, spacing_sq)
    current = smooth(current, source, spacing_sq, NU, layout)
    residue = source - operate(current, spacing_sq, layout)
    correction = vcycle(level_index + 1, None, restrict(residue), layout, gather_level)
    current = current + prolong(correction)
    return smooth(current, source, spacing_sq, NU, layout)


def shards(
    valence,
    start_potential,
    atom_tiles,
    atom_home,
    atom_offset_x,
    atom_offset_y,
    atom_offset_z,
    atom_size,
):
    domain_count = lax.axis_size("dom")
    group_count = lax.axis_size("grp")
    device_count = domain_count * group_count
    atoms_here = atom_tiles.shape[0]
    tile_cells = atom_tiles.shape[1]
    capacity = 2 * atoms_here // device_count
    tile_index = jnp.arange(TE, dtype=jnp.int32)
    inside = tile_index[None, :] < atom_size
    inside_cube = inside[:, :, None, None] & inside[:, None, :, None] & inside[:, None, None, :]
    masked = atom_tiles * inside_cube.reshape(atom_tiles.shape).astype(jnp.float32)
    targets = jnp.arange(device_count, dtype=jnp.int32)
    matches = (atom_home == targets[None, :]).astype(jnp.int32)
    before = jnp.cumsum(matches, axis=0) - matches
    slot_rank = jnp.sum(before * matches, axis=1)
    slot_index = atom_home[:, 0] * capacity + slot_rank
    offsets = jnp.concatenate([atom_offset_x, atom_offset_y, atom_offset_z], axis=1)
    send_tiles = (
        jnp.zeros((device_count * capacity, tile_cells), jnp.float32).at[slot_index].set(masked)
    )
    send_offsets = jnp.zeros((device_count * capacity, 3), jnp.int32).at[slot_index].set(offsets)
    got_tiles, got_offsets = (
        lax.all_to_all(
            send_tiles.reshape(device_count, capacity, tile_cells),
            ("dom", "grp"),
            split_axis=0,
            concat_axis=0,
            tiled=True,
        ),
        lax.all_to_all(
            send_offsets.reshape(device_count, capacity, 3),
            ("dom", "grp"),
            split_axis=0,
            concat_axis=0,
            tiled=True,
        ),
    )
    got_tiles = got_tiles.reshape(-1, tile_cells)
    got_offsets = got_offsets.reshape(-1, 3)
    slot_count = got_tiles.shape[0]
    width_x, width_y, width_z = valence.shape
    cells_x = got_offsets[:, 0:1] + tile_index[None, :]
    cells_y = (got_offsets[:, 1:2] + tile_index[None, :]) % width_y
    cells_z = got_offsets[:, 2:3] + tile_index[None, :]
    tile_shape = (slot_count, TE, TE, TE)
    index_x = jnp.broadcast_to(cells_x[:, :, None, None], tile_shape)
    index_y = jnp.broadcast_to(cells_y[:, None, :, None], tile_shape)
    index_z = jnp.broadcast_to(cells_z[:, None, None, :], tile_shape)
    deposit_grid = (
        jnp.zeros((width_x + TE, width_y, width_z), jnp.float32)
        .at[index_x, index_y, index_z]
        .add(got_tiles.reshape(tile_shape))
    )
    spill_planes = deposit_grid[width_x:]
    incoming = from_behind(spill_planes, "dom", 1)
    local_grid = deposit_grid[:width_x].at[:TE].add(incoming)
    density = valence + local_grid
    gather_level = 2
    potential = vcycle(0, start_potential, density, "split", gather_level)
    padded = neighbours(potential, "split")
    grad_x = 0.5 * (padded[2:, :, 1:-1] - padded[:-2, :, 1:-1])
    grad_y = 0.5 * (jnp.roll(potential, -1, axis=1) - jnp.roll(potential, 1, axis=1))
    grad_z = 0.5 * (padded[1:-1, :, 2:] - padded[1:-1, :, :-2])
    local_totals = jnp.stack(
        [
            jnp.sum(grad_x * grad_x),
            jnp.sum(grad_y * grad_y),
            jnp.sum(grad_z * grad_z),
            jnp.sum(grad_y * grad_z),
            jnp.sum(grad_x * grad_z),
            jnp.sum(grad_x * grad_y),
            jnp.sum(potential * density),
        ]
    )
    totals = lax.psum(local_totals, ("dom", "grp"))
    cell_count = width_x * width_y * width_z * device_count
    products = totals[:6] / cell_count
    energy = 0.5 * totals[6] / cell_count
    diagonal_mask = jnp.array([1.0, 1.0, 1.0, 0.0, 0.0, 0.0], jnp.float32)
    stress = products - energy * diagonal_mask
    return (potential, stress)


def solution(mesh):
    in_specs = (
        P("dom", None, "grp"),
        P("dom", None, "grp"),
        P(("dom", "grp"), None),
        P(("dom", "grp"), None),
        P(("dom", "grp"), None),
        P(("dom", "grp"), None),
        P(("dom", "grp"), None),
        P(("dom", "grp"), None),
    )
    out_specs = (P("dom", None, "grp"), P())
    return jax.shard_map(shards, mesh=mesh, in_specs=in_specs, out_specs=out_specs, check_vma=False)
```

profile of v0, /device:TPU:0, one launch (start us, length us, event | category | flops | bytes accessed | tf_op | source)
XLA Modules:
  0.0 2191.2 jit_solution(5525647373930291238)
XLA Ops:
  6.6 7.3 all-to-all-start
  28.5 7.9 all-to-all-start.1
  38.5 13.5 copy.45
  52.0 11.8 reshape.444
  65.2 1787.4 %scatter_custom_fusion.2 = f32[131072]{0:T(1024)S(1)} fusion(s32[262144]{0:T(1024)S(1)} %reshape.444, f32[262144]{0:T(1024)} %bitcast.79, f32[]{:T(128)} %constant.184.clone.1), kind=kCustom, calls=%fused_computation.131 | custom fusion | flops 262144 | bytes 524800
  1857.8 4.8 collective-permute-start.4
  1862.7 5.9 collective-permute-done.3
  1877.7 5.2 collective-permute-start.8
  1883.0 6.1 collective-permute-done.7
  1900.0 5.2 collective-permute-start.12
  1911.7 18.1 reshape.416
  1929.8 7.0 reduce_sum.103
  1968.4 15.2 all_gather.6
  1983.7 16.6 all_gather.7
  2000.7 9.8 reshape.418
  2020.4 6.9 reshape.419
  2050.4 5.0 collective-permute-start.28
  2057.7 6.5 broadcast_in_dim.114
  2064.2 12.6 reshape.421
  2096.6 5.4 collective-permute-start.34
  2104.3 4.7 collective-permute-start.36
  2115.2 7.5 collective-permute-start.38
  2125.1 4.7 collective-permute-start.40
  2139.9 49.5 %psum.7 = f32[7]{0:T(128)S(1)} all-reduce(f32[7]{0:T(128)S(1)} %stack.31), channel_id=1, replica_groups=mesh['dom'=8,'grp'=4] {'dom','grp'}, use_global_device_ids=true, to_apply=%region_16.17 | all-reduce | flops 7 | bytes 56 | tf_op jit(solution)/shard_map/psum | solution.py:213
  (238 shorter events, 163.9 us)
Async XLA Ops:
  6.6 21.9 all-to-all-start
  14.7 49.1 %collective-permute-start.2 = (f32[1,64,128]{2,1,0:T(8,128)S(1)}, f32[1,64,128]{2,1,0:T(8,128)S(1)}, u32[]{:S(2)}, u32[]{:S(2)}) collective-permute-start(f32[1,64,128]{2,1,0:T(8,128)S(1)} %get-tuple-element.80), channel_id=1, source_target_pairs={{0,4},{4,8},{8,12},{12,16},{16,20},{20,24},{24,28},{1,5},{5,9},{9,... | collective-permute-start | bytes 98312 | tf_op jit(solution)/shard_map/ppermute | solution.py:20
  16.8 47.0 %collective-permute-start.1 = (f32[1,64,128]{2,1,0:T(8,128)S(1)}, f32[1,64,128]{2,1,0:T(8,128)S(1)}, u32[]{:S(2)}, u32[]{:S(2)}) collective-permute-start(f32[1,64,128]{2,1,0:T(8,128)S(1)} %get-tuple-element.79), channel_id=1, source_target_pairs={{4,0},{8,4},{12,8},{16,12},{20,16},{24,20},{28,24},{5,1},{9,5},{13... | collective-permute-start | bytes 98312 | tf_op jit(solution)/shard_map/ppermute | solution.py:21
  28.5 35.4 %all-to-all-start.1 = ((f32[32,16,512]{2,1,0:T(8,128)}), f32[32,16,512]{2,1,0:T(8,128)S(1)}, u32[]{:S(2)}, u32[]{:S(2)}) async-start(f32[32,16,512]{2,1,0:T(8,128)} %bitcast.11), calls=%async_computation.1 | async-start | bytes 2097152 | tf_op jit(solution)/shard_map/all_to_all | solution.py:161
  1852.6 17.1 collective-permute-start
  1856.5 12.0 collective-permute-start.3
  1857.8 11.9 collective-permute-start.4
  1876.4 12.7 collective-permute-start.7
  1877.7 13.1 collective-permute-start.8
  1898.7 10.9 collective-permute-start.11
  1900.0 11.4 collective-permute-start.12
  1944.7 7.1 collective-permute-start.16
  1958.9 6.9 collective-permute-start.20
  2036.4 7.3 collective-permute-start.24
  2049.1 6.9 collective-permute-start.27
  2050.4 7.2 collective-permute-start.28
  2083.7 9.6 collective-permute-start.31
  2085.0 10.0 collective-permute-start.32
  2103.0 9.1 collective-permute-start.35
  2104.3 9.3 collective-permute-start.36
  2113.9 8.9 collective-permute-start.37
  2115.2 8.4 collective-permute-start.38
  2123.8 9.1 collective-permute-start.39
  2125.1 9.3 collective-permute-start.40
  (30 other events, 302.4 us)
where the time goes:
time: 2190 us
  other arithmetic  1810 us (83%)
  starting transfers between devices  132 us (6%)
  local copies, waits for them, and re-layouts  105 us (5%)
  blocking collectives  81.3 us (4%)
  waiting for transfers between devices  55 us (3%)
    unnamed x4, other arithmetic  1790 us
    ppermute x20, starting transfers between devices, extended(): before = lax.ppermute(last, axis, up)  87 us
    psum x1, blocking collectives, shards(): totals = lax.psum(local_totals, ('dom', 'grp'))  49.5 us
  transfers between devices with their start and end apart: 43, of which 29 were waited for; matrix products, arithmetic and copies ran while one was open for 2% of the time, Pallas kernels for 0%

commit v1 on v0

--- a/solution.py
+++ b/solution.py
@@ -1,7 +1,10 @@
 import jax
 import jax.numpy as jnp
 from jax import lax
+from jax.experimental import pallas as pl
+from jax.experimental.pallas import tpu as pltpu
 from jax.sharding import PartitionSpec as P
+import functools
 
 TE = 8
 NU = 2
@@ -125,6 +128,67 @@
     correction = vcycle(level_index + 1, None, restrict(residue), layout, gather_level)
     current = current + prolong(correction)
     return smooth(current, source, spacing_sq, NU, layout)
+
+
+ACCS = 4
+OFFSET_ROWS = 8
+
+
+def deposit_kernel(capacity, offsets_ref, tiles_ref, out_ref, *grids):
+    slots = offsets_ref.shape[0] // 3
+    width_y = out_ref.shape[1]
+    lane = lax.broadcasted_iota(jnp.int32, (TE, 128), 1)
+    low, high = (lane // TE == TE - 1, lane // TE == 2 * TE - 1)
+    for grid in grids:
+        grid[...] = jnp.zeros_like(grid)
+
+    def step(i, carry):
+        for j, grid in enumerate(grids):
+            slot = i * len(grids) + j
+            device = slot // capacity
+            first = (slot % capacity) * 4
+            at_x = offsets_ref[slot]
+            at_y = width_y - offsets_ref[slots + slot]
+            at_z = offsets_ref[2 * slots + slot]
+            parts = []
+            for q in range(4):
+                line = tiles_ref[device, pl.ds(first + q, 1), :]
+                line = jnp.broadcast_to(line, (TE, 128))
+                line = pltpu.roll(line, 0, 1, stride=TE, stride_axis=0)
+                for mask, shift in ((low, (at_z + 72) % 128), (high, (at_z + 8) % 128)):
+                    kept = jnp.where(mask, line, 0.0)
+                    parts.append(pltpu.roll(kept, shift, 1))
+            for a, part in enumerate(parts):
+                spot = (at_x + a, pl.ds(at_y, TE), slice(None))
+                grid[spot] = grid[spot] + part
+        return carry
+
+    lax.fori_loop(0, slots // len(grids), step, 0)
+    total = grids[0][...]
+    for grid in grids[1:]:
+        total = total + grid[...]
+    rows = width_y + TE
+    held = lax.broadcasted_iota(jnp.int32, (width_y, rows), 1)
+    wanted = lax.broadcasted_iota(jnp.int32, (width_y, rows), 0)
+    fold = ((rows - 1 - held) % width_y == wanted).astype(jnp.float32)
+    for x in range(out_ref.shape[0]):
+        out_ref[x] = jnp.dot(
+            fold, total[x], precision=lax.Precision.HIGHEST, preferred_element_type=jnp.float32
+        )
+
+
+def deposit(tiles, offsets, capacity, extent):
+    width_x, width_y, width_z = extent
+    vmem = pl.BlockSpec(memory_space=pltpu.VMEM)
+    return pl.pallas_call(
+        functools.partial(deposit_kernel, capacity),
+        out_shape=jax.ShapeDtypeStruct((width_x + TE, width_y, width_z), jnp.float32),
+        in_specs=[pl.BlockSpec(memory_space=pltpu.SMEM), vmem],
+        out_specs=vmem,
+        scratch_shapes=[pltpu.VMEM((width_x + TE, width_y + TE, width_z), jnp.float32)] * ACCS,
+        compiler_params=pltpu.CompilerParams(vmem_limit_bytes=32 * 1024 * 1024),
+        name="deposit",
+    )(offsets, tiles)
 
 
 def shards(
@@ -153,42 +217,18 @@
     slot_rank = jnp.sum(before * matches, axis=1)
     slot_index = atom_home[:, 0] * capacity + slot_rank
     offsets = jnp.concatenate([atom_offset_x, atom_offset_y, atom_offset_z], axis=1)
-    send_tiles = (
-        jnp.zeros((device_count * capacity, tile_cells), jnp.float32).at[slot_index].set(masked)
-    )
-    send_offsets = jnp.zeros((device_count * capacity, 3), jnp.int32).at[slot_index].set(offsets)
-    got_tiles, got_offsets = (
-        lax.all_to_all(
-            send_tiles.reshape(device_count, capacity, tile_cells),
-            ("dom", "grp"),
-            split_axis=0,
-            concat_axis=0,
-            tiled=True,
-        ),
-        lax.all_to_all(
-            send_offsets.reshape(device_count, capacity, 3),
-            ("dom", "grp"),
-            split_axis=0,
-            concat_axis=0,
-            tiled=True,
-        ),
-    )
-    got_tiles = got_tiles.reshape(-1, tile_cells)
-    got_offsets = got_offsets.reshape(-1, 3)
-    slot_count = got_tiles.shape[0]
+    slots = device_count * capacity
+    send_tiles = jnp.zeros((slots, tile_cells), jnp.float32).at[slot_index].set(masked)
+    send_offsets = jnp.zeros((slots, 3), jnp.float32).at[slot_index].set(offsets.astype(jnp.float32))
+    send_offsets = send_offsets.reshape(device_count, capacity, 3).transpose(0, 2, 1)
+    send_offsets = jnp.pad(send_offsets, ((0, 0), (0, OFFSET_ROWS - 3), (0, 128 - capacity)))
+    tile_rows = capacity * tile_cells // 128
+    send = jnp.concatenate([send_tiles.reshape(device_count, tile_rows, 128), send_offsets], axis=1)
+    got = lax.all_to_all(send, ("dom", "grp"), split_axis=0, concat_axis=0, tiled=True)
+    got_offsets = got[:, tile_rows : tile_rows + 3, :capacity].transpose(1, 0, 2)
+    got_offsets = got_offsets.reshape(-1).astype(jnp.int32)
     width_x, width_y, width_z = valence.shape
-    cells_x = got_offsets[:, 0:1] + tile_index[None, :]
-    cells_y = (got_offsets[:, 1:2] + tile_index[None, :]) % width_y
-    cells_z = got_offsets[:, 2:3] + tile_index[None, :]
-    tile_shape = (slot_count, TE, TE, TE)
-    index_x = jnp.broadcast_to(cells_x[:, :, None, None], tile_shape)
-    index_y = jnp.broadcast_to(cells_y[:, None, :, None], tile_shape)
-    index_z = jnp.broadcast_to(cells_z[:, None, None, :], tile_shape)
-    deposit_grid = (
-        jnp.zeros((width_x + TE, width_y, width_z), jnp.float32)
-        .at[index_x, index_y, index_z]
-        .add(got_tiles.reshape(tile_shape))
-    )
+    deposit_grid = deposit(got, got_offsets, capacity, valence.shape)
     spill_planes = deposit_grid[width_x:]
     incoming = from_behind(spill_planes, "dom", 1)
     local_grid = deposit_grid[:width_x].at[:TE].add(incoming)

time: 2190 us -> 411 us (0.19)
  other arithmetic: 1810 us -> 25.3 us
  local copies, waits for them, and re-layouts: 105 us -> 76.1 us
  Pallas kernels: 0 us -> 23.3 us
    unnamed x4 -> x0, other arithmetic: 1790 us -> none
    unnamed x28 -> x37, local copies, waits for them, and re-layouts: 27.9 us -> 2.64 us
    pallas_call x0 -> x1, Pallas kernels: none -> 23.3 us  [deposit(): pl.pallas_call(functools.partial(deposit_kernel, capacity), out_shape=jax...]
  transfers between devices with their start and end apart: 43 -> 42, of which waited for: 29 -> 30; matrix products, arithmetic and copies ran while one was open for 2% -> 1% of each run, Pallas kernels for 0% -> 0%
where the time goes in v1:
time: 411 us; the launch traced here: 409 us
  starting transfers between devices  124 us (30%)
  blocking collectives  81.2 us (20%)
  local copies, waits for them, and re-layouts  76.1 us (19%)
  waiting for transfers between devices  74.5 us (18%)
  other arithmetic  25.3 us (6%)
  Pallas kernels  23.3 us (6%)
    ppermute x20, starting transfers between devices, extended(): before = lax.ppermute(last, axis, up)  87.5 us
    psum x1, blocking collectives, shards(): totals = lax.psum(local_totals, ('dom', 'grp'))  49.4 us
    ppermute x20, waiting for transfers between devices, extended(): after = lax.ppermute(leading, axis, down)  31.8 us
    reshape x3, local copies, waits for them, and re-layouts, restrict(): residue.reshape(dims_now[0] // 2, 2, dims_now[1] // 2, 2, dims_now[2] //...  30 us
    ppermute x20, starting transfers between devices, extended(): after = lax.ppermute(leading, axis, down)  25.8 us
    pallas_call x1, Pallas kernels, deposit(): pl.pallas_call(functools.partial(deposit_kernel, capacity), out_shape=jax...  23.3 us
    ppermute x20, waiting for transfers between devices, extended(): before = lax.ppermute(last, axis, up)  22.1 us
    reshape x3, local copies, waits for them, and re-layouts, prolong(): return spread.reshape(dims_now[0] * 2, dims_now[1] * 2, dims_now[2] * 2)  21.2 us
  transfers between devices with their start and end apart: 42, of which 30 were waited for; matrix products, arithmetic and copies ran while one was open for 1% of the time, Pallas kernels for 0%

profile of v1, /device:TPU:0, one launch (start us, length us, event | category | flops | bytes accessed | tf_op | source)
XLA Modules:
  0.0 408.9 jit_solution(17274713280101195520)
XLA Ops:
  11.1 7.3 %all-to-all-start = ((f32[32,72,128]{2,1,0:T(8,128)}), f32[32,72,128]{2,1,0:T(8,128)S(1)}, u32[]{:S(2)}, u32[]{:S(2)}) async-start(f32[32,72,128]{2,1,0:T(8,128)} %select_maximum_fusion), calls=%async_computation | async-start | bytes 2359296 | tf_op jit(solution)/shard_map/all_to_all | solution.py:227
  25.5 20.7 %all-to-all-done.tiles_ref = f32[32,72,128]{2,1,0:T(8,128)S(1)} async-done(((f32[32,72,128]{2,1,0:T(8,128)}), f32[32,72,128]{2,1,0:T(8,128)S(1)}, u32[]{:S(2)}, u32[]{:S(2)}) %all-to-all-start) | async-done | bytes 1179680 | tf_op jit(solution)/shard_map/all_to_all | solution.py:227
  46.3 23.3 %deposit.1 = f32[16,64,128]{2,1,0:T(8,128)S(1)} custom-call(s32[1536]{0:T(1024)S(1)} %convert_element_type.48.offsets_ref, f32[32,72,128]{2,1,0:T(8,128)S(1)} %all-to-all-done.tiles_ref), custom_call_target="tpu_custom_call" | custom-call | tf_op jit(solution)/shard_map/deposit/pallas_call | solution.py:183
  80.4 5.1 %collective-permute-done.3 = f32[10,64,1]{2,1,0:T(8,128)S(1)} collective-permute-done((f32[10,64,1]{2,1,0:T(8,128)S(1)}, f32[10,64,1]{2,1,0:T(8,128)S(1)}, u32[]{:S(2)}, u32[]{:S(2)}) %collective-permute-start.3) | collective-permute-done | bytes 2592 | tf_op jit(solution)/shard_map/ppermute | solution.py:24
  95.4 5.0 %collective-permute-start.8 = (f32[10,64,1]{2,1,0:T(8,128)S(1)}, f32[10,64,1]{2,1,0:T(8,128)S(1)}, u32[]{:S(2)}, u32[]{:S(2)}) collective-permute-start(f32[10,64,1]{2,1,0:T(8,128)S(1)} %get-tuple-element.40), channel_id=1, source_target_pairs={{0,1},{1,2},{2,3},{4,5},{5,6},{6,7},{8,9},{9,10},{10,11},{12,13},{... | collective-permute-start | bytes 7688 | tf_op jit(solution)/shard_map/ppermute | solution.py:23
  100.4 5.5 %collective-permute-done.7 = f32[10,64,1]{2,1,0:T(8,128)S(1)} collective-permute-done((f32[10,64,1]{2,1,0:T(8,128)S(1)}, f32[10,64,1]{2,1,0:T(8,128)S(1)}, u32[]{:S(2)}, u32[]{:S(2)}) %collective-permute-start.7) | collective-permute-done | bytes 2592 | tf_op jit(solution)/shard_map/ppermute | solution.py:24
  117.6 5.0 %collective-permute-start.12 = (f32[10,64,1]{2,1,0:T(8,128)S(1)}, f32[10,64,1]{2,1,0:T(8,128)S(1)}, u32[]{:S(2)}, u32[]{:S(2)}) collective-permute-start(f32[10,64,1]{2,1,0:T(8,128)S(1)} %get-tuple-element.38), channel_id=1, source_target_pairs={{0,1},{1,2},{2,3},{4,5},{5,6},{6,7},{8,9},{9,10},{10,11},{12,13},{... | collective-permute-start | bytes 7688 | tf_op jit(solution)/shard_map/ppermute | solution.py:23
  129.2 18.1 %reshape.333 = f32[4,2,32,2,64,2]{5,4,3,2,1,0:T(8,128)} reshape(f32[8,64,128]{2,1,0:T(8,128)S(1)} %fusion.27) | data formatting | bytes 524288 | tf_op jit(solution)/shard_map/reshape | solution.py:102
  147.3 7.0 %reduce_sum.103 = f32[4,32,64]{2,1,0:T(8,128)S(1)} reduce(f32[4,2,32,2,64,2]{5,4,3,2,1,0:T(8,128)} %reshape.333, f32[]{:T(128)} %constant.167.clone.1), dimensions={1,3,5}, to_apply=%region_5.6 | reduce | flops 57344 | bytes 294916 | tf_op jit(solution)/shard_map/reduce_sum | solution.py:103
  162.3 4.7 %collective-permute-start.16 = (f32[6,32,1]{2,1,0:T(8,128)S(1)}, f32[6,32,1]{2,1,0:T(8,128)S(1)}, u32[]{:S(2)}, u32[]{:S(2)}) collective-permute-start(f32[6,32,1]{2,1,0:T(8,128)S(1)} %get-tuple-element.104), channel_id=1, source_target_pairs={{0,1},{1,2},{2,3},{4,5},{5,6},{6,7},{8,9},{9,10},{10,11},{12,13},{... | collective-permute-start | bytes 2312 | tf_op jit(solution)/shard_map/ppermute | solution.py:23
  176.8 4.6 %collective-permute-start.20 = (f32[6,32,1]{2,1,0:T(8,128)S(1)}, f32[6,32,1]{2,1,0:T(8,128)S(1)}, u32[]{:S(2)}, u32[]{:S(2)}) collective-permute-start(f32[6,32,1]{2,1,0:T(8,128)S(1)} %get-tuple-element.102), channel_id=1, source_target_pairs={{0,1},{1,2},{2,3},{4,5},{5,6},{6,7},{8,9},{9,10},{10,11},{12,13},{... | collective-permute-start | bytes 2312 | tf_op jit(solution)/shard_map/ppermute | solution.py:23
  186.3 15.0 %all_gather.6 = f32[2,16,128]{1,0,2:T(2,128)S(1)} all-gather(f32[2,16,32]{1,0,2:T(2,128)S(1)} %copy.40), channel_id=1, replica_groups=mesh['dom'=8,'grp'=4] {'grp'}, dimensions={2}, use_global_device_ids=true | all-gather | bytes 20480 | tf_op jit(solution)/shard_map/all_gather | solution.py:116
  201.3 16.8 %all_gather.7 = f32[16,16,128]{2,1,0:T(8,128)S(1)} all-gather(f32[2,16,128]{2,1,0:T(8,128)S(1)} %copy.41), channel_id=1, replica_groups=mesh['dom'=8,'grp'=4] {'dom'}, dimensions={0}, use_global_device_ids=true | all-gather | bytes 147456 | tf_op jit(solution)/shard_map/all_gather | solution.py:117
  218.5 9.8 %reshape.335 = f32[8,2,8,2,64,2]{5,4,3,2,1,0:T(8,128)} reshape(f32[16,16,128]{2,1,0:T(8,128)S(1)} %fusion.69) | data formatting | bytes 262144 | tf_op jit(solution)/shard_map/reshape | solution.py:102
  238.2 6.9 %reshape.336 = f32[16,16,128]{2,1,0:T(8,128)S(1)} reshape(f32[8,2,8,2,64,2]{5,4,3,2,1,0:T(8,128)} %broadcast_in_dim.33) | data formatting | bytes 262144 | tf_op jit(solution)/shard_map/reshape | solution.py:111
  268.2 5.0 %collective-permute-start.28 = (f32[6,32,1]{2,1,0:T(8,128)S(1)}, f32[6,32,1]{2,1,0:T(8,128)S(1)}, u32[]{:S(2)}, u32[]{:S(2)}) collective-permute-start(f32[6,32,1]{2,1,0:T(8,128)S(1)} %get-tuple-element.98), channel_id=1, source_target_pairs={{0,1},{1,2},{2,3},{4,5},{5,6},{6,7},{8,9},{9,10},{10,11},{12,13},{... | collective-permute-start | bytes 2312 | tf_op jit(solution)/shard_map/ppermute | solution.py:23
  275.5 6.5 %broadcast_in_dim.35 = f32[4,2,32,2,64,2]{5,4,3,2,1,0:T(8,128)} broadcast(f32[4,32,64]{2,1,0:T(8,128)S(1)} %fusion.91), dimensions={0,2,4} | broadcast | bytes 294912 | tf_op jit(solution)/shard_map/broadcast_in_dim | solution.py:108
  282.0 12.6 %reshape.338 = f32[8,64,128]{2,1,0:T(8,128)S(1)} reshape(f32[4,2,32,2,64,2]{5,4,3,2,1,0:T(8,128)} %broadcast_in_dim.35) | data formatting | bytes 524288 | tf_op jit(solution)/shard_map/reshape | solution.py:111
  302.8 4.7 %collective-permute-start.32 = (f32[10,64,1]{2,1,0:T(8,128)S(1)}, f32[10,64,1]{2,1,0:T(8,128)S(1)}, u32[]{:S(2)}, u32[]{:S(2)}) collective-permute-start(f32[10,64,1]{2,1,0:T(8,128)S(1)} %get-tuple-element.36), channel_id=1, source_target_pairs={{0,1},{1,2},{2,3},{4,5},{5,6},{6,7},{8,9},{9,10},{10,11},{12,13},{... | collective-permute-start | bytes 7688 | tf_op jit(solution)/shard_map/ppermute | solution.py:23
  314.5 5.4 %collective-permute-start.34 = (f32[1,64,128]{2,1,0:T(8,128)S(1)}, f32[1,64,128]{2,1,0:T(8,128)S(1)}, u32[]{:S(2)}, u32[]{:S(2)}) collective-permute-start(f32[1,64,128]{2,1,0:T(8,128)S(1)} %get-tuple-element.53), channel_id=1, source_target_pairs={{0,4},{4,8},{8,12},{12,16},{16,20},{20,24},{24,28},{1,5},{5,9},{9,... | collective-permute-start | bytes 98312 | tf_op jit(solution)/shard_map/ppermute | solution.py:23
  322.2 4.7 %collective-permute-start.36 = (f32[10,64,1]{2,1,0:T(8,128)S(1)}, f32[10,64,1]{2,1,0:T(8,128)S(1)}, u32[]{:S(2)}, u32[]{:S(2)}) collective-permute-start(f32[10,64,1]{2,1,0:T(8,128)S(1)} %get-tuple-element.34), channel_id=1, source_target_pairs={{0,1},{1,2},{2,3},{4,5},{5,6},{6,7},{8,9},{9,10},{10,11},{12,13},{... | collective-permute-start | bytes 7688 | tf_op jit(solution)/shard_map/ppermute | solution.py:23
  333.1 7.5 %collective-permute-start.38 = (f32[1,64,128]{2,1,0:T(8,128)S(1)}, f32[1,64,128]{2,1,0:T(8,128)S(1)}, u32[]{:S(2)}, u32[]{:S(2)}) collective-permute-start(f32[1,64,128]{2,1,0:T(8,128)S(1)} %get-tuple-element.44), channel_id=1, source_target_pairs={{0,4},{4,8},{8,12},{12,16},{16,20},{20,24},{24,28},{1,5},{5,9},{9,... | collective-permute-start | bytes 98312 | tf_op jit(solution)/shard_map/ppermute | solution.py:23
  342.9 4.7 %collective-permute-start.40 = (f32[10,64,1]{2,1,0:T(8,128)S(1)}, f32[10,64,1]{2,1,0:T(8,128)S(1)}, u32[]{:S(2)}, u32[]{:S(2)}) collective-permute-start(f32[10,64,1]{2,1,0:T(8,128)S(1)} %get-tuple-element.32), channel_id=1, source_target_pairs={{0,1},{1,2},{2,3},{4,5},{5,6},{6,7},{8,9},{9,10},{10,11},{12,13},{... | collective-permute-start | bytes 7688 | tf_op jit(solution)/shard_map/ppermute | solution.py:23
  357.7 49.4 %psum.7 = f32[7]{0:T(128)S(1)} all-reduce(f32[7]{0:T(128)S(1)} %stack.31), channel_id=1, replica_groups=mesh['dom'=8,'grp'=4] {'dom','grp'}, use_global_device_ids=true, to_apply=%region_15.16 | all-reduce | flops 7 | bytes 56 | tf_op jit(solution)/shard_map/psum | solution.py:253
  (236 shorter events, 151.0 us)
Async XLA Ops:
  11.1 35.1 %all-to-all-start = ((f32[32,72,128]{2,1,0:T(8,128)}), f32[32,72,128]{2,1,0:T(8,128)S(1)}, u32[]{:S(2)}, u32[]{:S(2)}) async-start(f32[32,72,128]{2,1,0:T(8,128)} %select_maximum_fusion), calls=%async_computation | async-start | bytes 2359296 | tf_op jit(solution)/shard_map/all_to_all | solution.py:227
  18.4 7.0 %collective-permute-start.2 = (f32[1,64,128]{2,1,0:T(8,128)S(1)}, f32[1,64,128]{2,1,0:T(8,128)S(1)}, u32[]{:S(2)}, u32[]{:S(2)}) collective-permute-start(f32[1,64,128]{2,1,0:T(8,128)S(1)} %get-tuple-element.78), channel_id=1, source_target_pairs={{0,4},{4,8},{8,12},{12,16},{16,20},{20,24},{24,28},{1,5},{5,9},{9,... | collective-permute-start | bytes 98312 | tf_op jit(solution)/shard_map/ppermute | solution.py:23
  70.3 16.4 %collective-permute-start = (f32[8,64,128]{2,1,0:T(8,128)}, f32[8,64,128]{2,1,0:T(8,128)S(1)}, u32[]{:S(2)}, u32[]{:S(2)}) collective-permute-start(f32[8,64,128]{2,1,0:T(8,128)} %slice.710), channel_id=1, source_target_pairs={{0,4},{4,8},{8,12},{12,16},{16,20},{20,24},{24,28},{1,5},{5,9},{9,... | collective-permute-start | bytes 786440 | tf_op jit(solution)/shard_map/ppermute | solution.py:32
  74.0 11.5 %collective-permute-start.3 = (f32[10,64,1]{2,1,0:T(8,128)S(1)}, f32[10,64,1]{2,1,0:T(8,128)S(1)}, u32[]{:S(2)}, u32[]{:S(2)}) collective-permute-start(f32[10,64,1]{2,1,0:T(8,128)S(1)} %get-tuple-element.41), channel_id=1, source_target_pairs={{1,0},{2,1},{3,2},{5,4},{6,5},{7,6},{9,8},{10,9},{11,10},{13,12},{... | collective-permute-start | bytes 7688 | tf_op jit(solution)/shard_map/ppermute | solution.py:24
  75.3 11.4 %collective-permute-start.4 = (f32[10,64,1]{2,1,0:T(8,128)S(1)}, f32[10,64,1]{2,1,0:T(8,128)S(1)}, u32[]{:S(2)}, u32[]{:S(2)}) collective-permute-start(f32[10,64,1]{2,1,0:T(8,128)S(1)} %get-tuple-element.42), channel_id=1, source_target_pairs={{0,1},{1,2},{2,3},{4,5},{5,6},{6,7},{8,9},{9,10},{10,11},{12,13},{... | collective-permute-start | bytes 7688 | tf_op jit(solution)/shard_map/ppermute | solution.py:23
  94.1 11.9 %collective-permute-start.7 = (f32[10,64,1]{2,1,0:T(8,128)S(1)}, f32[10,64,1]{2,1,0:T(8,128)S(1)}, u32[]{:S(2)}, u32[]{:S(2)}) collective-permute-start(f32[10,64,1]{2,1,0:T(8,128)S(1)} %get-tuple-element.39), channel_id=1, source_target_pairs={{1,0},{2,1},{3,2},{5,4},{6,5},{7,6},{9,8},{10,9},{11,10},{13,12},{... | collective-permute-start | bytes 7688 | tf_op jit(solution)/shard_map/ppermute | solution.py:24
  95.4 12.4 %collective-permute-start.8 = (f32[10,64,1]{2,1,0:T(8,128)S(1)}, f32[10,64,1]{2,1,0:T(8,128)S(1)}, u32[]{:S(2)}, u32[]{:S(2)}) collective-permute-start(f32[10,64,1]{2,1,0:T(8,128)S(1)} %get-tuple-element.40), channel_id=1, source_target_pairs={{0,1},{1,2},{2,3},{4,5},{5,6},{6,7},{8,9},{9,10},{10,11},{12,13},{... | collective-permute-start | bytes 7688 | tf_op jit(solution)/shard_map/ppermute | solution.py:23
  116.3 10.9 %collective-permute-start.11 = (f32[10,64,1]{2,1,0:T(8,128)S(1)}, f32[10,64,1]{2,1,0:T(8,128)S(1)}, u32[]{:S(2)}, u32[]{:S(2)}) collective-permute-start(f32[10,64,1]{2,1,0:T(8,128)S(1)} %get-tuple-element.37), channel_id=1, source_target_pairs={{1,0},{2,1},{3,2},{5,4},{6,5},{7,6},{9,8},{10,9},{11,10},{13,12},{... | collective-permute-start | bytes 7688 | tf_op jit(solution)/shard_map/ppermute | solution.py:24
  117.6 11.4 %collective-permute-start.12 = (f32[10,64,1]{2,1,0:T(8,128)S(1)}, f32[10,64,1]{2,1,0:T(8,128)S(1)}, u32[]{:S(2)}, u32[]{:S(2)}) collective-permute-start(f32[10,64,1]{2,1,0:T(8,128)S(1)} %get-tuple-element.38), channel_id=1, source_target_pairs={{0,1},{1,2},{2,3},{4,5},{5,6},{6,7},{8,9},{9,10},{10,11},{12,13},{... | collective-permute-start | bytes 7688 | tf_op jit(solution)/shard_map/ppermute | solution.py:23
  162.3 6.9 %collective-permute-start.16 = (f32[6,32,1]{2,1,0:T(8,128)S(1)}, f32[6,32,1]{2,1,0:T(8,128)S(1)}, u32[]{:S(2)}, u32[]{:S(2)}) collective-permute-start(f32[6,32,1]{2,1,0:T(8,128)S(1)} %get-tuple-element.104), channel_id=1, source_target_pairs={{0,1},{1,2},{2,3},{4,5},{5,6},{6,7},{8,9},{9,10},{10,11},{12,13},{... | collective-permute-start | bytes 2312 | tf_op jit(solution)/shard_map/ppermute | solution.py:23
  176.8 6.8 %collective-permute-start.20 = (f32[6,32,1]{2,1,0:T(8,128)S(1)}, f32[6,32,1]{2,1,0:T(8,128)S(1)}, u32[]{:S(2)}, u32[]{:S(2)}) collective-permute-start(f32[6,32,1]{2,1,0:T(8,128)S(1)} %get-tuple-element.102), channel_id=1, source_target_pairs={{0,1},{1,2},{2,3},{4,5},{5,6},{6,7},{8,9},{9,10},{10,11},{12,13},{... | collective-permute-start | bytes 2312 | tf_op jit(solution)/shard_map/ppermute | solution.py:23
  252.9 6.8 %collective-permute-start.23 = (f32[6,32,1]{2,1,0:T(8,128)S(1)}, f32[6,32,1]{2,1,0:T(8,128)S(1)}, u32[]{:S(2)}, u32[]{:S(2)}) collective-permute-start(f32[6,32,1]{2,1,0:T(8,128)S(1)} %get-tuple-element.99), channel_id=1, source_target_pairs={{1,0},{2,1},{3,2},{5,4},{6,5},{7,6},{9,8},{10,9},{11,10},{13,12},{... | collective-permute-start | bytes 2312 | tf_op jit(solution)/shard_map/ppermute | solution.py:24
  254.2 7.3 %collective-permute-start.24 = (f32[6,32,1]{2,1,0:T(8,128)S(1)}, f32[6,32,1]{2,1,0:T(8,128)S(1)}, u32[]{:S(2)}, u32[]{:S(2)}) collective-permute-start(f32[6,32,1]{2,1,0:T(8,128)S(1)} %get-tuple-element.100), channel_id=1, source_target_pairs={{0,1},{1,2},{2,3},{4,5},{5,6},{6,7},{8,9},{9,10},{10,11},{12,13},{... | collective-permute-start | bytes 2312 | tf_op jit(solution)/shard_map/ppermute | solution.py:23
  266.9 6.9 %collective-permute-start.27 = (f32[6,32,1]{2,1,0:T(8,128)S(1)}, f32[6,32,1]{2,1,0:T(8,128)S(1)}, u32[]{:S(2)}, u32[]{:S(2)}) collective-permute-start(f32[6,32,1]{2,1,0:T(8,128)S(1)} %get-tuple-element.97), channel_id=1, source_target_pairs={{1,0},{2,1},{3,2},{5,4},{6,5},{7,6},{9,8},{10,9},{11,10},{13,12},{... | collective-permute-start | bytes 2312 | tf_op jit(solution)/shard_map/ppermute | solution.py:24
  268.2 7.2 %collective-permute-start.28 = (f32[6,32,1]{2,1,0:T(8,128)S(1)}, f32[6,32,1]{2,1,0:T(8,128)S(1)}, u32[]{:S(2)}, u32[]{:S(2)}) collective-permute-start(f32[6,32,1]{2,1,0:T(8,128)S(1)} %get-tuple-element.98), channel_id=1, source_target_pairs={{0,1},{1,2},{2,3},{4,5},{5,6},{6,7},{8,9},{9,10},{10,11},{12,13},{... | collective-permute-start | bytes 2312 | tf_op jit(solution)/shard_map/ppermute | solution.py:23
  301.5 9.6 %collective-permute-start.31 = (f32[10,64,1]{2,1,0:T(8,128)S(1)}, f32[10,64,1]{2,1,0:T(8,128)S(1)}, u32[]{:S(2)}, u32[]{:S(2)}) collective-permute-start(f32[10,64,1]{2,1,0:T(8,128)S(1)} %get-tuple-element.35), channel_id=1, source_target_pairs={{1,0},{2,1},{3,2},{5,4},{6,5},{7,6},{9,8},{10,9},{11,10},{13,12},{... | collective-permute-start | bytes 7688 | tf_op jit(solution)/shard_map/ppermute | solution.py:24
  302.8 10.0 %collective-permute-start.32 = (f32[10,64,1]{2,1,0:T(8,128)S(1)}, f32[10,64,1]{2,1,0:T(8,128)S(1)}, u32[]{:S(2)}, u32[]{:S(2)}) collective-permute-start(f32[10,64,1]{2,1,0:T(8,128)S(1)} %get-tuple-element.36), channel_id=1, source_target_pairs={{0,1},{1,2},{2,3},{4,5},{5,6},{6,7},{8,9},{9,10},{10,11},{12,13},{... | collective-permute-start | bytes 7688 | tf_op jit(solution)/shard_map/ppermute | solution.py:23
  313.2 6.7 %collective-permute-start.33 = (f32[1,64,128]{2,1,0:T(8,128)S(1)}, f32[1,64,128]{2,1,0:T(8,128)S(1)}, u32[]{:S(2)}, u32[]{:S(2)}) collective-permute-start(f32[1,64,128]{2,1,0:T(8,128)S(1)} %get-tuple-element.54), channel_id=1, source_target_pairs={{4,0},{8,4},{12,8},{16,12},{20,16},{24,20},{28,24},{5,1},{9,5},{13... | collective-permute-start | bytes 98312 | tf_op jit(solution)/shard_map/ppermute | solution.py:24
  320.9 9.1 %collective-permute-start.35 = (f32[10,64,1]{2,1,0:T(8,128)S(1)}, f32[10,64,1]{2,1,0:T(8,128)S(1)}, u32[]{:S(2)}, u32[]{:S(2)}) collective-permute-start(f32[10,64,1]{2,1,0:T(8,128)S(1)} %get-tuple-element.33), channel_id=1, source_target_pairs={{1,0},{2,1},{3,2},{5,4},{6,5},{7,6},{9,8},{10,9},{11,10},{13,12},{... | collective-permute-start | bytes 7688 | tf_op jit(solution)/shard_map/ppermute | solution.py:24
  322.2 9.3 %collective-permute-start.36 = (f32[10,64,1]{2,1,0:T(8,128)S(1)}, f32[10,64,1]{2,1,0:T(8,128)S(1)}, u32[]{:S(2)}, u32[]{:S(2)}) collective-permute-start(f32[10,64,1]{2,1,0:T(8,128)S(1)} %get-tuple-element.34), channel_id=1, source_target_pairs={{0,1},{1,2},{2,3},{4,5},{5,6},{6,7},{8,9},{9,10},{10,11},{12,13},{... | collective-permute-start | bytes 7688 | tf_op jit(solution)/shard_map/ppermute | solution.py:23
  331.8 8.9 %collective-permute-start.37 = (f32[1,64,128]{2,1,0:T(8,128)S(1)}, f32[1,64,128]{2,1,0:T(8,128)S(1)}, u32[]{:S(2)}, u32[]{:S(2)}) collective-permute-start(f32[1,64,128]{2,1,0:T(8,128)S(1)} %get-tuple-element.43), channel_id=1, source_target_pairs={{4,0},{8,4},{12,8},{16,12},{20,16},{24,20},{28,24},{5,1},{9,5},{13... | collective-permute-start | bytes 98312 | tf_op jit(solution)/shard_map/ppermute | solution.py:24
  333.1 8.4 %collective-permute-start.38 = (f32[1,64,128]{2,1,0:T(8,128)S(1)}, f32[1,64,128]{2,1,0:T(8,128)S(1)}, u32[]{:S(2)}, u32[]{:S(2)}) collective-permute-start(f32[1,64,128]{2,1,0:T(8,128)S(1)} %get-tuple-element.44), channel_id=1, source_target_pairs={{0,4},{4,8},{8,12},{12,16},{16,20},{20,24},{24,28},{1,5},{5,9},{9,... | collective-permute-start | bytes 98312 | tf_op jit(solution)/shard_map/ppermute | solution.py:23
  341.6 9.1 %collective-permute-start.39 = (f32[10,64,1]{2,1,0:T(8,128)S(1)}, f32[10,64,1]{2,1,0:T(8,128)S(1)}, u32[]{:S(2)}, u32[]{:S(2)}) collective-permute-start(f32[10,64,1]{2,1,0:T(8,128)S(1)} %get-tuple-element.31), channel_id=1, source_target_pairs={{1,0},{2,1},{3,2},{5,4},{6,5},{7,6},{9,8},{10,9},{11,10},{13,12},{... | collective-permute-start | bytes 7688 | tf_op jit(solution)/shard_map/ppermute | solution.py:24
  342.9 9.3 %collective-permute-start.40 = (f32[10,64,1]{2,1,0:T(8,128)S(1)}, f32[10,64,1]{2,1,0:T(8,128)S(1)}, u32[]{:S(2)}, u32[]{:S(2)}) collective-permute-start(f32[10,64,1]{2,1,0:T(8,128)S(1)} %get-tuple-element.32), channel_id=1, source_target_pairs={{0,1},{1,2},{2,3},{4,5},{5,6},{6,7},{8,9},{9,10},{10,11},{12,13},{... | collective-permute-start | bytes 7688 | tf_op jit(solution)/shard_map/ppermute | solution.py:23
  (35 other events, 246.5 us)

commit v2 on v1

v2 whole, which is shorter than its diff:
```python
import jax
import jax.numpy as jnp
from jax import lax
from jax.experimental import pallas as pl
from jax.experimental.pallas import tpu as pltpu
from jax.sharding import PartitionSpec as P
import functools
import numpy as np

TE = 8
HALO = 3
HIGHEST = lax.Precision.HIGHEST


ACCS = 4
OFFSET_ROWS = 8


def deposit_kernel(capacity, offsets_ref, tiles_ref, out_ref, *grids):
    slots = offsets_ref.shape[0] // 3
    width_y = out_ref.shape[1]
    lane = lax.broadcasted_iota(jnp.int32, (TE, 128), 1)
    low, high = (lane // TE == TE - 1, lane // TE == 2 * TE - 1)
    for grid in grids:
        grid[...] = jnp.zeros_like(grid)

    def step(i, carry):
        for j, grid in enumerate(grids):
            slot = i * len(grids) + j
            device = slot // capacity
            first = (slot % capacity) * 4
            at_x = offsets_ref[slot]
            at_y = width_y - offsets_ref[slots + slot]
            at_z = offsets_ref[2 * slots + slot]
            parts = []
            for q in range(4):
                line = tiles_ref[device, pl.ds(first + q, 1), :]
                line = jnp.broadcast_to(line, (TE, 128))
                line = pltpu.roll(line, 0, 1, stride=TE, stride_axis=0)
                for mask, shift in ((low, (at_z + 72) % 128), (high, (at_z + 8) % 128)):
                    kept = jnp.where(mask, line, 0.0)
                    parts.append(pltpu.roll(kept, shift, 1))
            for a, part in enumerate(parts):
                spot = (at_x + a, pl.ds(at_y, TE), slice(None))
                grid[spot] = grid[spot] + part
        return carry

    lax.fori_loop(0, slots // len(grids), step, 0)
    total = grids[0][...]
    for grid in grids[1:]:
        total = total + grid[...]
    rows = width_y + TE
    held = lax.broadcasted_iota(jnp.int32, (width_y, rows), 1)
    wanted = lax.broadcasted_iota(jnp.int32, (width_y, rows), 0)
    fold = ((rows - 1 - held) % width_y == wanted).astype(jnp.float32)
    for x in range(out_ref.shape[0]):
        out_ref[x] = jnp.dot(
            fold, total[x], precision=lax.Precision.HIGHEST, preferred_element_type=jnp.float32
        )


def deposit(tiles, offsets, capacity, extent):
    width_x, width_y, width_z = extent
    vmem = pl.BlockSpec(memory_space=pltpu.VMEM)
    return pl.pallas_call(
        functools.partial(deposit_kernel, capacity),
        out_shape=jax.ShapeDtypeStruct((width_x + TE, width_y, width_z), jnp.float32),
        in_specs=[pl.BlockSpec(memory_space=pltpu.SMEM), vmem],
        out_specs=vmem,
        scratch_shapes=[pltpu.VMEM((width_x + TE, width_y + TE, width_z), jnp.float32)] * ACCS,
        compiler_params=pltpu.CompilerParams(vmem_limit_bytes=32 * 1024 * 1024),
        name="deposit",
    )(offsets, tiles)


def sine_table(length):
    steps = np.arange(length) + 1.0
    table = np.sqrt(2.0 / (length + 1)) * np.sin(np.pi * np.outer(steps, steps) / (length + 1))
    return table, 2.0 - 2.0 * np.cos(np.pi * steps / (length + 1))


def cyclic_table(length):
    steps = np.arange(length)[:, None]
    column = np.arange(length)[None, :]
    freqs = (column + 1) // 2
    angles = 2.0 * np.pi * freqs * steps / length
    use_sine = (column % 2 == 0) & (column > 0)
    edges = (column == 0) | (column == length - 1)
    scales = np.where(edges, np.sqrt(1.0 / length), np.sqrt(2.0 / length))
    table = scales * np.where(use_sine, np.sin(angles), np.cos(angles))
    return table, 2.0 - 2.0 * np.cos(2.0 * np.pi * freqs[0] / length)


def pooling(fine, rows=None, columns=None):
    table = np.zeros((rows or fine, columns or fine // 2))
    table[np.arange(fine), np.arange(fine) // 2] = 1.0
    return table


def tables(doms, grps, extent):
    cx, ny, cz = extent
    x2, y2, z2 = doms * cx // 4, ny // 4, grps * cz // 4
    table_x, values_x = sine_table(x2 // 2)
    table_y, values_y = cyclic_table(y2 // 2)
    table_z, values_z = sine_table(z2 // 2)
    plane = np.kron(table_x, table_y)
    pool_xy = np.kron(pooling(x2), pooling(y2))
    pool_z = pooling(z2)
    values = values_x[:, None, None] + values_y[None, :, None] + values_z[None, None, :]
    cells = cz // 4
    spread = np.zeros((z2, cz))
    spread[np.arange(cz // 2) // 2, np.arange(cz // 2)] = 1.0
    spread[cells, cz // 2 : cz // 2 + 2] = 1.0
    spread[z2 - 1, cz - 2 :] = 1.0
    found = (
        pooling(cz, cz, cz) / 8.0,
        pooling(ny).T,
        pooling(cz // 2, cz, cz) / 8.0,
        pooling(ny // 2).T,
        (pool_xy @ plane).T / 4.0,
        pool_z @ table_z / 2.0,
        64.0 / values.reshape(-1, z2 // 2),
        pool_xy @ plane,
        (pool_z @ table_z).T,
        spread,
        pooling(ny // 2),
        pooling(cz, cz, cz).T,
        pooling(ny),
    )
    return [jnp.asarray(table, jnp.float32) for table in found]


def matmul(a, b):
    return jnp.dot(a, b, precision=HIGHEST, preferred_element_type=jnp.float32)


CORNERS = ((0, 1), (0, -1), (1, 1), (1, -1), (-1, 1), (-1, -1))


def grid_kernel(
    doms, grps,
    deposit_ref, valence_ref, start_ref,
    rz1, ry1, rz2, ry2, into_xy, into_z, inverse, from_xy, from_z, pz2, py2, pz1, py1,
    potential_ref, totals_ref,
    ua, ub, fe, spill, second, edge, faces, sides, f1, edge1, faces1, sides1, va, vb, ge,
    whole_f, wa, wb, pieces, sums,
    spill_sem, ex_send, ex_recv, ex1_send, ex1_recv, all_send, all_recv,
):
    n = doms * grps
    dom, grp = lax.axis_index("dom"), lax.axis_index("grp")
    me = dom * grps + grp
    cx, ny, cz = valence_ref.shape
    h = HALO

    def at(dx, dz):
        return (lax.rem(dom + dx + doms, doms), lax.rem(grp + dz + grps, grps))

    def nth(k):
        t = lax.rem(me + k, n)
        return (t // grps, lax.rem(t, grps))

    barrier = pltpu.get_barrier_semaphore()

    def greet(k, carry):
        pl.semaphore_signal(barrier, inc=1, device_id=nth(k), device_id_type=pl.DeviceIdType.MESH)
        return carry

    lax.fori_loop(1, n, greet, 0)
    pl.semaphore_wait(barrier, n - 1)

    def send(src, dst, send_sem, recv_sem, target):
        return pltpu.make_async_remote_copy(
            src_ref=src, dst_ref=dst, send_sem=send_sem, recv_sem=recv_sem,
            device_id=target, device_id_type=pl.DeviceIdType.MESH,
        )

    def exchange(src, planes, packed, faces_to, sides_to, send_sem, recv_sem):
        copies = [
            send(packed, sides_to.at[k], send_sem.at[k], recv_sem.at[k], at(*CORNERS[k]))
            for k in range(6)
        ]
        for k, (first, dx) in enumerate(((planes - h, 1), (0, -1))):
            part = src.at[pl.ds(first, h)]
            copies.append(send(part, faces_to.at[k], send_sem.at[6 + k], recv_sem.at[6 + k], at(dx, 0)))
        for copy in copies:
            copy.start()
        return copies

    def all_send_to(buf, which):
        def one(k):
            return send(buf.at[me], buf.at[me], all_send.at[which, k], all_recv.at[which, k], nth(k))

        def go(k, carry):
            one(k).start()
            return carry

        def done(k, carry):
            one(k).wait()
            return carry

        lax.fori_loop(1, n, go, 0)
        lax.fori_loop(1, n, done, 0)

    lane = lax.broadcasted_iota(jnp.int32, (1, cz), 1)
    edge_lane = (lane < h) | (lane >= cz - h)
    has_up = (grp < grps - 1).astype(jnp.float32)
    has_down = (grp > 0).astype(jnp.float32)
    beside = jnp.where(lane < h, has_up, 0.0) + jnp.where(lane >= cz - h, has_down, 0.0)
    lanes0 = jnp.concatenate([jnp.ones((1, cz), jnp.float32), beside], axis=1)
    half = cz // 2
    lanes1 = (
        jnp.where(lane < half, 1.0, 0.0)
        + jnp.where((lane >= half) & (lane < half + h), has_up, 0.0)
        + jnp.where(lane >= cz - h, has_down, 0.0)
    )

    def inside(plane, count):
        x = dom * count + plane - h
        return ((x >= 0) & (x < doms * count)).astype(jnp.float32)

    def pack0(src, which):
        total = jnp.zeros((ny, cz), jnp.float32)
        for x in range(cx):
            kept = jnp.where(edge_lane, src[x], 0.0)
            total = total + (kept if x == 0 else pltpu.roll(kept, 16 * x, 1))
        edge[which] = total

    def widen0(src, which, dst):
        from_up = lane % 16 < 8
        kinds = ((3, 2, 0, cx - h, 0), (1, 0, None, 0, h), (5, 4, 1, 0, cx + h))
        for up, down, face, first, place in kinds:
            mixed = jnp.where(from_up, sides[which, up], sides[which, down])
            for i in range(cx if face is None else h):
                x = first + i
                own = src[x] if face is None else faces[which, face, i]
                far = mixed if x == 0 else pltpu.roll(mixed, cz - 16 * x, 1)
                mask = inside(place + i, cx)
                dst[place + i, :, 0:cz] = own * mask
                dst[place + i, :, cz : 2 * cz] = far * (beside * mask)

    def around(u, p, axis_y, axis_z):
        c = u[p]
        total = u[p - 1] + u[p + 1]
        total = total + pltpu.roll(c, 1, 0) + pltpu.roll(c, axis_y - 1, 0)
        return c, total + pltpu.roll(c, 1, 1) + pltpu.roll(c, axis_z - 1, 1)

    def sweep0(src, dst, first, last):
        def one(p, carry):
            c, near = around(src, p, ny, 2 * cz)
            new = c * (1.0 / 3.0) + (fe[p] + near) * (1.0 / 9.0)
            dst[p] = new * (lanes0 * inside(p, cx))
            return carry

        lax.fori_loop(first, last, one, 0)

    pack0(start_ref, 0)
    going_u = exchange(start_ref, cx, edge.at[0], faces.at[0], sides.at[0], ex_send.at[0], ex_recv.at[0])
    spilling = send(
        deposit_ref.at[pl.ds(cx, cx)], spill, spill_sem.at[0], spill_sem.at[1], at(1, 0)
    )
    spilling.start()
    spilling.wait()
    inner = (dom > 0).astype(jnp.float32)
    for x in range(cx):
        second[0, x] = valence_ref[x] + (deposit_ref[x] + spill[x] * inner)
    density = second.at[0]
    pack0(density, 1)
    going_f = exchange(density, cx, edge.at[1], faces.at[1], sides.at[1], ex_send.at[1], ex_recv.at[1])
    for copy in going_u:
        copy.wait()
    widen0(start_ref, 0, ua)
    for copy in going_f:
        copy.wait()
    widen0(density, 1, fe)

    sweep0(ua, ub, 1, cx + 2 * h - 1)
    sweep0(ub, ua, 2, cx + 2 * h - 2)
    for i in range(cx // 2):
        both = jnp.zeros((ny, cz), jnp.float32)
        for p in (h + 2 * i, h + 2 * i + 1):
            c, near = around(ua, p, ny, 2 * cz)
            both = both + (fe[p] + near - 6.0 * c)[:, 0:cz]
        f1[i] = matmul(ry1[...], matmul(both, rz1[...]))

    c1, y1 = cx // 2, ny // 2
    total = jnp.zeros((y1, cz), jnp.float32)
    edge_lane1 = (lane < h) | ((lane >= half - h) & (lane < half))
    for x in range(c1):
        kept = jnp.where(edge_lane1, f1[x], 0.0)
        total = total + (kept if x == 0 else pltpu.roll(kept, 8 * x, 1))
    edge1[...] = total
    for copy in exchange(f1, c1, edge1, faces1, sides1, ex1_send, ex1_recv):
        copy.wait()
    from_up = lane < 40
    for up, down, face, first, place in ((3, 2, 0, c1 - h, 0), (1, 0, None, 0, h), (5, 4, 1, 0, c1 + h)):
        mixed = jnp.where(from_up, sides1[up], sides1[down])
        for i in range(c1 if face is None else h):
            x = first + i
            own = f1[x] if face is None else faces1[face, i]
            far = pltpu.roll(mixed, half - 8 * x, 1)
            value = jnp.where(lane < half, own, far) * (lanes1 * inside(place + i, c1))
            ge[place + i] = value
            va[place + i] = value * (4.0 / 9.0)

    def sweep1(src, dst, first, last):
        for p in range(first, last):
            c, near = around(src, p, y1, cz)
            new = c * (1.0 / 3.0) + near * (1.0 / 9.0) + ge[p] * (4.0 / 9.0)
            dst[p] = new * (lanes1 * inside(p, c1))

    sweep1(va, vb, 1, c1 + 2 * h - 1)
    packed = jnp.zeros((8, cz), jnp.float32)
    for i in range(c1 // 2):
        both = jnp.zeros((y1, cz), jnp.float32)
        for p in (h + 2 * i, h + 2 * i + 1):
            c, near = around(vb, p, y1, cz)
            both = both + (ge[p] + (near - 6.0 * c) * 0.25)
        f2 = matmul(ry2[...], matmul(both, rz2[...]))
        for k in range(2):
            j = 2 * i + k
            rows = f2[8 * k : 8 * k + 8]
            packed = packed + (rows if j == 0 else pltpu.roll(rows, 32 * j, 1))
    pieces[me] = packed
    all_send_to(pieces, 0)

    planes, y2 = 2 * doms, ny // 4
    z2 = grps * 32
    for j in range(4):
        for t in range(grps // 4):
            def unpack(d, carry):
                line = jnp.zeros((8, cz), jnp.float32)
                for g in range(4):
                    shift = 32 * ((g - j) % 4)
                    piece = pieces[d * grps + 4 * t + g]
                    piece = piece if shift == 0 else pltpu.roll(piece, shift, 1)
                    line = line + jnp.where(lane // 32 == g, piece, 0.0)
                whole_f[2 * d + j // 2, 8 * (j % 2) : 8 * (j % 2) + 8, cz * t : cz * t + cz] = line
                return carry

            lax.fori_loop(0, doms, unpack, 0)
    lane2 = lax.broadcasted_iota(jnp.int32, (1, 1, z2), 2)
    zero_plane = jnp.zeros((y2, z2), jnp.float32)
    for w in (wa, wb):
        w[0] = zero_plane
        w[planes + 1] = zero_plane

    def around2(w):
        c = w[1 : planes + 1]
        near = w[0:planes] + w[2 : planes + 2]
        near = near + pltpu.roll(c, 1, 1) + pltpu.roll(c, y2 - 1, 1)
        near = near + jnp.where(lane2 == 0, 0.0, pltpu.roll(c, 1, 2))
        return c, near + jnp.where(lane2 == z2 - 1, 0.0, pltpu.roll(c, z2 - 1, 2))

    def sweep2(src, dst):
        c, near = around2(src)
        dst[1 : planes + 1] = c * (1.0 / 3.0) + near * (1.0 / 9.0) + whole_f[...] * (16.0 / 9.0)

    wa[1 : planes + 1] = whole_f[...] * (16.0 / 9.0)
    sweep2(wa, wb)
    c, near = around2(wb)
    residue = whole_f[...] + (near - 6.0 * c) * (1.0 / 16.0)
    modes = matmul(matmul(into_xy[...], residue.reshape(planes * y2, z2)), into_z[...])
    back = matmul(matmul(from_xy[...], modes * inverse[...]), from_z[...])
    wb[1 : planes + 1] = c + back.reshape(planes, y2, z2)
    sweep2(wb, wa)
    sweep2(wa, wb)

    for i in range(c1 // 2 + 2):
        plane = wb[2 * dom + i]
        plane = pltpu.roll(plane, lax.rem(z2 - 32 * grp, z2), 1)
        fine = matmul(py2[...], matmul(plane, pz2[...]))
        for p in (2 * i + 1, 2 * i + 2):
            va[p] = (vb[p] + fine) * (lanes1 * inside(p, c1))
    sweep1(va, vb, 2, c1 + 2 * h - 2)
    sweep1(vb, va, 3, c1 + 2 * h - 3)

    for i in range(c1):
        fine = matmul(py1[...], matmul(va[h + i], pz1[...]))
        for x in (2 * i, 2 * i + 1):
            second[1, x] = ua[h + x, :, 0:cz] + fine
    update = second.at[1]
    pack0(update, 2)
    for copy in exchange(update, cx, edge.at[2], faces.at[2], sides.at[2], ex_send.at[2], ex_recv.at[2]):
        copy.wait()
    widen0(update, 2, ua)
    sweep0(ua, ub, 1, cx + 2 * h - 1)
    sweep0(ub, ua, 2, cx + 2 * h - 2)

    def grads(x, carry):
        p = x + h
        c = ua[p]
        own = c[:, 0:cz]
        potential_ref[x] = own
        grad_x = 0.5 * (ua[p + 1, :, 0:cz] - ua[p - 1, :, 0:cz])
        grad_y = 0.5 * (pltpu.roll(own, ny - 1, 0) - pltpu.roll(own, 1, 0))
        grad_z = 0.5 * (pltpu.roll(c, 2 * cz - 1, 1) - pltpu.roll(c, 1, 1))[:, 0:cz]
        pairs = (
            (grad_x, grad_x), (grad_y, grad_y), (grad_z, grad_z), (grad_y, grad_z),
            (grad_x, grad_z), (grad_x, grad_y), (own, density[x]),
        )
        return tuple(
            old + jnp.sum((a * b).reshape(ny // 8, 8, cz), axis=0)
            for old, (a, b) in zip(carry, pairs)
        )

    start = tuple(jnp.zeros((8, cz), jnp.float32) for _ in range(7))
    found = lax.fori_loop(0, cx, grads, start)
    sums[me] = jnp.concatenate(
        [jnp.sum(value, axis=0, keepdims=True) for value in found]
        + [jnp.zeros((1, cz), jnp.float32)], axis=0
    )
    all_send_to(sums, 1)
    totals_ref[...] = jnp.sum(sums[...], axis=0)


def solve_grid(deposit_grid, valence, start_potential):
    doms, grps = lax.axis_size("dom"), lax.axis_size("grp")
    n = doms * grps
    cx, ny, cz = valence.shape
    h = HALO
    c1, y1, y2, z2 = cx // 2, ny // 2, ny // 4, grps * cz // 4
    vmem = pl.BlockSpec(memory_space=pltpu.VMEM)
    constants = tables(doms, grps, valence.shape)

    def buf(*shape):
        return pltpu.VMEM(shape, jnp.float32)

    wide = buf(cx + 2 * h, ny, 2 * cz)
    wide1 = buf(c1 + 2 * h, y1, cz)
    whole = buf(2 * doms + 2, y2, z2)
    dma = pltpu.SemaphoreType.DMA
    return pl.pallas_call(
        functools.partial(grid_kernel, doms, grps),
        out_shape=(
            jax.ShapeDtypeStruct(valence.shape, jnp.float32),
            jax.ShapeDtypeStruct((8, cz), jnp.float32),
        ),
        in_specs=[vmem] * (3 + len(constants)),
        out_specs=(vmem, vmem),
        scratch_shapes=[
            wide, wide, wide, buf(cx, ny, cz), buf(2, cx, ny, cz),
            buf(3, ny, cz), buf(3, 2, h, ny, cz), buf(3, 6, ny, cz),
            buf(c1, y1, cz), buf(y1, cz), buf(2, h, y1, cz), buf(6, y1, cz),
            wide1, wide1, wide1,
            buf(2 * doms, y2, z2), whole, whole, buf(n, 8, cz), buf(n, 8, cz),
            dma((2,)), dma((3, 8)), dma((3, 8)), dma((8,)), dma((8,)), dma((2, n)), dma((2, n)),
        ],
        compiler_params=pltpu.CompilerParams(
            collective_id=0, has_side_effects=True, vmem_limit_bytes=48 * 1024 * 1024
        ),
        name="grid",
    )(deposit_grid, valence, start_potential, *constants)


def shards(
    valence,
    start_potential,
    atom_tiles,
    atom_home,
    atom_offset_x,
    atom_offset_y,
    atom_offset_z,
    atom_size,
):
    domain_count = lax.axis_size("dom")
    group_count = lax.axis_size("grp")
    device_count = domain_count * group_count
    atoms_here = atom_tiles.shape[0]
    tile_cells = atom_tiles.shape[1]
    capacity = 2 * atoms_here // device_count
    tile_index = jnp.arange(TE, dtype=jnp.int32)
    inside = tile_index[None, :] < atom_size
    inside_cube = inside[:, :, None, None] & inside[:, None, :, None] & inside[:, None, None, :]
    masked = atom_tiles * inside_cube.reshape(atom_tiles.shape).astype(jnp.float32)
    targets = jnp.arange(device_count, dtype=jnp.int32)
    matches = (atom_home == targets[None, :]).astype(jnp.int32)
    before = jnp.cumsum(matches, axis=0) - matches
    slot_rank = jnp.sum(before * matches, axis=1)
    slot_index = atom_home[:, 0] * capacity + slot_rank
    offsets = jnp.concatenate([atom_offset_x, atom_offset_y, atom_offset_z], axis=1)
    slots = device_count * capacity
    send_tiles = jnp.zeros((slots, tile_cells), jnp.float32).at[slot_index].set(masked)
    send_offsets = jnp.zeros((slots, 3), jnp.float32).at[slot_index].set(offsets.astype(jnp.float32))
    send_offsets = send_offsets.reshape(device_count, capacity, 3).transpose(0, 2, 1)
    send_offsets = jnp.pad(send_offsets, ((0, 0), (0, OFFSET_ROWS - 3), (0, 128 - capacity)))
    tile_rows = capacity * tile_cells // 128
    send = jnp.concatenate([send_tiles.reshape(device_count, tile_rows, 128), send_offsets], axis=1)
    got = lax.all_to_all(send, ("dom", "grp"), split_axis=0, concat_axis=0, tiled=True)
    got_offsets = got[:, tile_rows : tile_rows + 3, :capacity].transpose(1, 0, 2)
    got_offsets = got_offsets.reshape(-1).astype(jnp.int32)
    width_x, width_y, width_z = valence.shape
    deposit_grid = deposit(got, got_offsets, capacity, valence.shape)
    potential, partial = solve_grid(deposit_grid, valence, start_potential)
    totals = jnp.sum(partial[:7], axis=1)
    cell_count = width_x * width_y * width_z * device_count
    products = totals[:6] / cell_count
    energy = 0.5 * totals[6] / cell_count
    diagonal_mask = jnp.array([1.0, 1.0, 1.0, 0.0, 0.0, 0.0], jnp.float32)
    stress = products - energy * diagonal_mask
    return (potential, stress)


def solution(mesh):
    in_specs = (
        P("dom", None, "grp"),
        P("dom", None, "grp"),
        P(("dom", "grp"), None),
        P(("dom", "grp"), None),
        P(("dom", "grp"), None),
        P(("dom", "grp"), None),
        P(("dom", "grp"), None),
        P(("dom", "grp"), None),
    )
    out_specs = (P("dom", None, "grp"), P())
    return jax.shard_map(shards, mesh=mesh, in_specs=in_specs, out_specs=out_specs, check_vma=False)
```

time: 411 us -> 129 us (0.31)
  starting transfers between devices: 124 us -> 0 us
  waiting for transfers between devices: 74.5 us -> 0 us
  local copies, waits for them, and re-layouts: 76.1 us -> 5.42 us
  Pallas kernels: 23.3 us -> 79.1 us
  blocking collectives: 81.2 us -> 37.2 us
  other arithmetic: 25.3 us -> 5.13 us
    ppermute x41 -> x0, starting transfers between devices: 117 us -> none  [the longest x20 87.5 us: extended(): before = lax.ppermute(last, axis, up)]
    pallas_call x0 -> x1, Pallas kernels: none -> 55.8 us  [solve_grid(): pl.pallas_call(functools.partial(grid_kernel, doms, grps), out_shape=(jax...]
    ppermute x41 -> x0, waiting for transfers between devices: 53.8 us -> none  [the longest x20 31.8 us: extended(): after = lax.ppermute(leading, axis, down)]
    reshape x6 -> x0, local copies, waits for them, and re-layouts: 51.2 us -> none  [the longest x3 30 us: restrict(): residue.reshape(dims_now[0] // 2, 2, dims_now[1] // 2, 2, dims_now[2] //...]
    psum x1 -> x0, blocking collectives: 49.4 us -> none  [shards(): totals = lax.psum(local_totals, ('dom', 'grp'))]
    all_to_all x0 -> x1, blocking collectives: none -> 37.2 us  [shards(): lax.all_to_all(send, ('dom', 'grp'), split_axis=0, concat_axis=0, tiled=T...]
    all_gather x2 -> x0, blocking collectives: 31.7 us -> none  [the longest x1 16.8 us: vcycle(): whole_grid = lax.all_gather(column, 'dom', axis=0, tiled=True)]
    all_to_all x1 -> x0, waiting for transfers between devices: 20.7 us -> none  [shards(): lax.all_to_all(send, ('dom', 'grp'), split_axis=0, concat_axis=0, tiled=T...]
  transfers between devices with their start and end apart: 42 -> 0, of which waited for: 30 -> 0; matrix products, arithmetic and copies ran while one was open for 1% -> 0% of each run, Pallas kernels for 0% -> 0%
where the time goes in v2:
time: 129 us
  Pallas kernels  79.1 us (61%)
  blocking collectives  37.2 us (29%)
  local copies, waits for them, and re-layouts  5.42 us (4%)
  other arithmetic  5.13 us (4%)
  between operations  1.62 us (1%)
    pallas_call x1, Pallas kernels, solve_grid(): pl.pallas_call(functools.partial(grid_kernel, doms, grps), out_shape=(jax...  55.8 us
    all_to_all x1, blocking collectives, shards(): lax.all_to_all(send, ('dom', 'grp'), split_axis=0, concat_axis=0, tiled=T...  37.2 us
    pallas_call x1, Pallas kernels, deposit(): pl.pallas_call(functools.partial(deposit_kernel, capacity), out_shape=jax...  23.3 us

profile of v2, /device:TPU:0, one launch (start us, length us, event | category | flops | bytes accessed | tf_op | source)
XLA Modules:
  0.0 128.5 jit_solution(12233434103239892132)
XLA Ops:
  0.6 0.7 iota_compare_fusion.3
  1.4 0.7 fusion.8
  2.1 0.6 reduce-window.6
  2.7 0.2 slice_reduce_fusion
  2.9 0.8 fusion.7
  3.7 0.7 compare_select_fusion
  4.4 0.1 broadcast_and_fusion
  4.4 0.7 add_convert_fusion
  5.2 0.1 copy.27
  5.3 1.2 scatter_custom_fusion.1
  6.5 0.2 copy.29
  6.8 0.2 copy.25
  7.0 0.1 bitcast_select_fusion
  7.1 0.2 copy.26
  7.3 1.7 %scatter_custom_fusion = f32[512,512]{1,0:T(8,128)S(1)} fusion(s32[256]{0:T(256)S(1)} %bitcast.40, f32[256,512]{1,0:T(8,128)S(1)} %copy.26, f32[]{:T(128)} %constant.23.clone.1), kind=kCustom, calls=%fused_computation.4 | custom fusion | bytes 1048580 | tf_op jit(solution)/shard_map/scatter | solution.py:482
  9.1 0.1 select_maximum_fusion
  9.2 37.2 %all_to_all.5.tiles_ref = f32[32,72,128]{2,1,0:T(8,128)S(1)} all-to-all(f32[32,72,128]{2,1,0:T(8,128)S(1)} %select_maximum_fusion), channel_id=1, replica_groups=mesh['dom'=8,'grp'=4] {'dom','grp'}, dimensions={0} | all-to-all | bytes 2359296 | tf_op jit(solution)/shard_map/all_to_all | solution.py:488
  46.6 0.1 convert_element_type.25.offsets_ref
  46.6 23.3 %deposit.1.deposit_ref = f32[16,64,128]{2,1,0:T(8,128)S(1)} custom-call(s32[1536]{0:T(1024)S(1)} %convert_element_type.25.offsets_ref, f32[32,72,128]{2,1,0:T(8,128)S(1)} %all_to_all.5.tiles_ref), custom_call_target="tpu_custom_call" | custom-call | tf_op jit(solution)/shard_map/deposit/pallas_call | solution.py:65
  70.1 55.8 %grid.1 = (f32[8,64,128]{2,1,0:T(8,128)S(1)}, f32[8,128]{1,0:T(8,128)S(1)}) custom-call(f32[16,64,128]{2,1,0:T(8,128)S(1)} %deposit.1.deposit_ref, f32[8,64,128]{2,1,0:T(8,128)S(1)} %copy-done, f32[8,64,128]{2,1,0:T(8,128)S(1)} %copy-done.1, f32[128,128]{1,0:T(8,128)S(1)} %copy-done.8, f32[32,64]{1,0:T(8,128)S(1)} %copy-done.13, f32[128,128]{1,0:T(8,128)S(1)} %copy-done.7, ...), custom_call_target="tpu_custom_call" | custom-call | tf_op jit(solution)/shard_map/grid/pallas_call | solution.py:432
  125.9 0.1 slice_reduce_fusion.1
  126.0 0.6 slice.23
  127.3 0.5 multiply_subtract_fusion
  127.8 0.7 copy.36
  (40 shorter events, 0.2 us)
Async XLA Ops:
  0.6 6.2 %copy-start.15 = (f32[256,512]{1,0:T(8,128)S(1)}, f32[256,512]{1,0:T(8,128)}, u32[]{:S(2)}) copy-start(f32[256,512]{1,0:T(8,128)} %param.24) | copy-start | bytes 1572868
  46.4 23.6 %copy-start = (f32[8,64,128]{2,1,0:T(8,128)S(1)}, f32[8,64,128]{2,1,0:T(8,128)}, u32[]{:S(2)}) copy-start(f32[8,64,128]{2,1,0:T(8,128)} %valence_ref.1) | copy-start | bytes 786436
  46.4 23.6 %copy-start.1 = (f32[8,64,128]{2,1,0:T(8,128)S(1)}, f32[8,64,128]{2,1,0:T(8,128)}, u32[]{:S(2)}) copy-start(f32[8,64,128]{2,1,0:T(8,128)} %start_ref.1) | copy-start | bytes 786436
  46.4 23.6 %copy-start.2 = (f32[256,64]{1,0:T(8,128)S(1)}, f32[256,64]{1,0:T(8,128)}, u32[]{:S(2)}) copy-start(f32[256,64]{1,0:T(8,128)} %constant.61.clone.from_xy) | copy-start | bytes 196612
  46.4 23.6 %copy-start.3 = (f32[128,128]{1,0:T(8,128)S(1)}, f32[128,128]{1,0:T(8,128)}, u32[]{:S(2)}) copy-start(f32[128,128]{1,0:T(8,128)} %constant.65.clone.pz1) | copy-start | bytes 196612
  46.4 23.6 %copy-start.4 = (f32[128,128]{1,0:T(8,128)S(1)}, f32[128,128]{1,0:T(8,128)}, u32[]{:S(2)}) copy-start(f32[128,128]{1,0:T(8,128)} %constant.63.clone.pz2) | copy-start | bytes 196612
  46.4 23.6 %copy-start.5 = (f32[128,64]{1,0:T(8,128)S(1)}, f32[128,64]{1,0:T(8,128)}, u32[]{:S(2)}) copy-start(f32[128,64]{1,0:T(8,128)} %constant.59.clone.into_z) | copy-start | bytes 98308
  46.4 23.6 %copy-start.6 = (f32[64,256]{1,0:T(8,128)S(1)}, f32[64,256]{1,0:T(8,128)}, u32[]{:S(2)}) copy-start(f32[64,256]{1,0:T(8,128)} %constant.58.clone.into_xy) | copy-start | bytes 196612
  46.4 23.6 %copy-start.7 = (f32[128,128]{1,0:T(8,128)S(1)}, f32[128,128]{1,0:T(8,128)}, u32[]{:S(2)}) copy-start(f32[128,128]{1,0:T(8,128)} %constant.56.clone.rz2) | copy-start | bytes 196612
  46.4 23.6 %copy-start.8 = (f32[128,128]{1,0:T(8,128)S(1)}, f32[128,128]{1,0:T(8,128)}, u32[]{:S(2)}) copy-start(f32[128,128]{1,0:T(8,128)} %constant.54.clone.rz1) | copy-start | bytes 196612
  46.5 23.6 %copy-start.9 = (f32[64,32]{1,0:T(8,128)S(1)}, f32[64,32]{1,0:T(8,128)}, u32[]{:S(2)}) copy-start(f32[64,32]{1,0:T(8,128)} %constant.66.clone.py1) | copy-start | bytes 24580
  46.5 23.6 %copy-start.10 = (f32[64,128]{1,0:T(8,128)S(1)}, f32[64,128]{1,0:T(8,128)}, u32[]{:S(2)}) copy-start(f32[64,128]{1,0:T(8,128)} %constant.62.clone.from_z) | copy-start | bytes 98308
  46.5 23.6 %copy-start.11 = (f32[64,64]{1,0:T(8,128)S(1)}, f32[64,64]{1,0:T(8,128)}, u32[]{:S(2)}) copy-start(f32[64,64]{1,0:T(8,128)} %constant.60.clone.inverse) | copy-start | bytes 49156
  46.5 23.6 %copy-start.12 = (f32[32,16]{1,0:T(8,128)S(1)}, f32[32,16]{1,0:T(8,128)}, u32[]{:S(2)}) copy-start(f32[32,16]{1,0:T(8,128)} %constant.64.clone.py2) | copy-start | bytes 6148
  46.5 23.6 %copy-start.13 = (f32[32,64]{1,0:T(8,128)S(1)}, f32[32,64]{1,0:T(8,128)}, u32[]{:S(2)}) copy-start(f32[32,64]{1,0:T(8,128)} %constant.55.clone.ry1) | copy-start | bytes 24580
  46.5 23.6 %copy-start.14 = (f32[16,32]{1,0:T(8,128)S(1)}, f32[16,32]{1,0:T(8,128)}, u32[]{:S(2)}) copy-start(f32[16,32]{1,0:T(8,128)} %constant.57.clone.ry2) | copy-start | bytes 6148
  70.1 57.2 %copy-start.16 = (f32[6]{0:T(128)S(1)}, f32[6]{0:T(128)}, u32[]{:S(2)}) copy-start(f32[6]{0:T(128)} %constant.67.clone) | copy-start | bytes 76

commit v3 on v2

--- a/solution.py
+++ b/solution.py
@@ -12,8 +12,93 @@
 HIGHEST = lax.Precision.HIGHEST
 
 
-ACCS = 4
+ACCS = 8
 OFFSET_ROWS = 8
+
+
+def parts_of(value):
+    high = value.astype(jnp.bfloat16)
+    rest = value - high.astype(jnp.float32)
+    middle = rest.astype(jnp.bfloat16)
+    low = (rest - middle.astype(jnp.float32)).astype(jnp.bfloat16)
+    return high, middle, low
+
+
+def times_right(rows, table):
+    count = rows.shape[0]
+    stacked = jnp.concatenate(parts_of(rows), axis=0)
+    out = jnp.dot(stacked, table.astype(jnp.bfloat16), preferred_element_type=jnp.float32)
+    return out[0:count] + (out[count : 2 * count] + out[2 * count : 3 * count])
+
+
+def times_left(table, columns):
+    count = columns.shape[1]
+    stacked = jnp.concatenate(parts_of(columns), axis=1)
+    out = jnp.dot(table.astype(jnp.bfloat16), stacked, preferred_element_type=jnp.float32)
+    return out[:, 0:count] + (out[:, count : 2 * count] + out[:, 2 * count : 3 * count])
+
+
+def resample(left, planes, right):
+    rows = planes[0].shape[0]
+    count, width = len(planes), right.shape[1]
+    along = times_right(jnp.concatenate(planes, axis=0), right)
+    beside = [along[rows * i : rows * i + rows] for i in range(count)]
+    out = times_left(left, jnp.concatenate(beside, axis=1))
+    return [out[:, width * i : width * i + width] for i in range(count)]
+
+
+def swap_kernel(doms, grps, send_ref, got_ref, send_sem, recv_sem):
+    n = doms * grps
+    me = lax.axis_index("dom") * grps + lax.axis_index("grp")
+
+    def copy_to(k):
+        t = lax.rem(me + k, n)
+        return pltpu.make_async_remote_copy(
+            src_ref=send_ref.at[t], dst_ref=got_ref.at[me],
+            send_sem=send_sem.at[k], recv_sem=recv_sem.at[k],
+            device_id=(t // grps, lax.rem(t, grps)), device_id_type=pl.DeviceIdType.MESH,
+        )
+
+    barrier = pltpu.get_barrier_semaphore()
+
+    def greet(k, carry):
+        t = lax.rem(me + k, n)
+        pl.semaphore_signal(
+            barrier, inc=1, device_id=(t // grps, lax.rem(t, grps)),
+            device_id_type=pl.DeviceIdType.MESH,
+        )
+        return carry
+
+    def go(k, carry):
+        copy_to(k).start()
+        return carry
+
+    def done(k, carry):
+        copy_to(k).wait()
+        return carry
+
+    lax.fori_loop(1, n, greet, 0)
+    pl.semaphore_wait(barrier, n - 1)
+    lax.fori_loop(1, n, go, 0)
+    got_ref[me] = send_ref[me]
+    lax.fori_loop(1, n, done, 0)
+
+
+def swap(send):
+    doms, grps = lax.axis_size("dom"), lax.axis_size("grp")
+    vmem = pl.BlockSpec(memory_space=pltpu.VMEM)
+    dma = pltpu.SemaphoreType.DMA
+    return pl.pallas_call(
+        functools.partial(swap_kernel, doms, grps),
+        out_shape=jax.ShapeDtypeStruct(send.shape, jnp.float32),
+        in_specs=[vmem],
+        out_specs=vmem,
+        scratch_shapes=[dma((doms * grps,)), dma((doms * grps,))],
+        compiler_params=pltpu.CompilerParams(
+            collective_id=1, has_side_effects=True, vmem_limit_bytes=32 * 1024 * 1024
+        ),
+        name="swap",
+    )(send)
 
 
 def deposit_kernel(capacity, offsets_ref, tiles_ref, out_ref, *grids):
@@ -30,7 +115,7 @@
             device = slot // capacity
             first = (slot % capacity) * 4
             at_x = offsets_ref[slot]
-            at_y = width_y - offsets_ref[slots + slot]
+            at_y = width_y + TE - offsets_ref[slots + slot]
             at_z = offsets_ref[2 * slots + slot]
             parts = []
             for q in range(4):
@@ -49,14 +134,15 @@
     total = grids[0][...]
     for grid in grids[1:]:
         total = total + grid[...]
-    rows = width_y + TE
+    rows = grids[0].shape[1]
     held = lax.broadcasted_iota(jnp.int32, (width_y, rows), 1)
     wanted = lax.broadcasted_iota(jnp.int32, (width_y, rows), 0)
     fold = ((rows - 1 - held) % width_y == wanted).astype(jnp.float32)
-    for x in range(out_ref.shape[0]):
-        out_ref[x] = jnp.dot(
-            fold, total[x], precision=lax.Precision.HIGHEST, preferred_element_type=jnp.float32
-        )
+    for first in range(0, out_ref.shape[0], 4):
+        planes = jnp.concatenate([total[first + i] for i in range(4)], axis=1)
+        folded = times_left(fold, planes)
+        for i in range(4):
+            out_ref[first + i] = folded[:, 128 * i : 128 * i + 128]
 
 
 def deposit(tiles, offsets, capacity, extent):
@@ -67,7 +153,7 @@
         out_shape=jax.ShapeDtypeStruct((width_x + TE, width_y, width_z), jnp.float32),
         in_specs=[pl.BlockSpec(memory_space=pltpu.SMEM), vmem],
         out_specs=vmem,
-        scratch_shapes=[pltpu.VMEM((width_x + TE, width_y + TE, width_z), jnp.float32)] * ACCS,
+        scratch_shapes=[pltpu.VMEM((width_x + TE, width_y + 2 * TE, width_z), jnp.float32)] * ACCS,
         compiler_params=pltpu.CompilerParams(vmem_limit_bytes=32 * 1024 * 1024),
         name="deposit",
     )(offsets, tiles)
@@ -275,12 +361,15 @@
 
     sweep0(ua, ub, 1, cx + 2 * h - 1)
     sweep0(ub, ua, 2, cx + 2 * h - 2)
+    residues = []
     for i in range(cx // 2):
         both = jnp.zeros((ny, cz), jnp.float32)
         for p in (h + 2 * i, h + 2 * i + 1):
             c, near = around(ua, p, ny, 2 * cz)
             both = both + (fe[p] + near - 6.0 * c)[:, 0:cz]
-        f1[i] = matmul(ry1[...], matmul(both, rz1[...]))
+        residues.append(both)
+    for i, plane in enumerate(resample(ry1[...], residues, rz1[...])):
+        f1[i] = plane
 
     c1, y1 = cx // 2, ny // 2
     total = jnp.zeros((y1, cz), jnp.float32)
@@ -310,12 +399,14 @@
 
     sweep1(va, vb, 1, c1 + 2 * h - 1)
     packed = jnp.zeros((8, cz), jnp.float32)
+    residues = []
     for i in range(c1 // 2):
         both = jnp.zeros((y1, cz), jnp.float32)
         for p in (h + 2 * i, h + 2 * i + 1):
             c, near = around(vb, p, y1, cz)
             both = both + (ge[p] + (near - 6.0 * c) * 0.25)
-        f2 = matmul(ry2[...], matmul(both, rz2[...]))
+        residues.append(both)
+    for i, f2 in enumerate(resample(ry2[...], residues, rz2[...])):
         for k in range(2):
             j = 2 * i + k
             rows = f2[8 * k : 8 * k + 8]
@@ -365,17 +456,16 @@
     sweep2(wb, wa)
     sweep2(wa, wb)
 
-    for i in range(c1 // 2 + 2):
-        plane = wb[2 * dom + i]
-        plane = pltpu.roll(plane, lax.rem(z2 - 32 * grp, z2), 1)
-        fine = matmul(py2[...], matmul(plane, pz2[...]))
+    shift = lax.rem(z2 - 32 * grp, z2)
+    coarse = [pltpu.roll(wb[2 * dom + i], shift, 1) for i in range(c1 // 2 + 2)]
+    for i, fine in enumerate(resample(py2[...], coarse, pz2[...])):
         for p in (2 * i + 1, 2 * i + 2):
             va[p] = (vb[p] + fine) * (lanes1 * inside(p, c1))
     sweep1(va, vb, 2, c1 + 2 * h - 2)
     sweep1(vb, va, 3, c1 + 2 * h - 3)
 
-    for i in range(c1):
-        fine = matmul(py1[...], matmul(va[h + i], pz1[...]))
+    coarse = [va[h + i] for i in range(c1)]
+    for i, fine in enumerate(resample(py1[...], coarse, pz1[...])):
         for x in (2 * i, 2 * i + 1):
             second[1, x] = ua[h + x, :, 0:cz] + fine
     update = second.at[1]
@@ -485,7 +575,7 @@
     send_offsets = jnp.pad(send_offsets, ((0, 0), (0, OFFSET_ROWS - 3), (0, 128 - capacity)))
     tile_rows = capacity * tile_cells // 128
     send = jnp.concatenate([send_tiles.reshape(device_count, tile_rows, 128), send_offsets], axis=1)
-    got = lax.all_to_all(send, ("dom", "grp"), split_axis=0, concat_axis=0, tiled=True)
+    got = swap(send)
     got_offsets = got[:, tile_rows : tile_rows + 3, :capacity].transpose(1, 0, 2)
     got_offsets = got_offsets.reshape(-1).astype(jnp.int32)
     width_x, width_y, width_z = valence.shape

time: 129 us -> 115 us (0.89)
  blocking collectives: 37.2 us -> 0 us
  Pallas kernels: 79.1 us -> 103 us
    all_to_all x1 -> x0, blocking collectives: 37.2 us -> none  [shards(): lax.all_to_all(send, ('dom', 'grp'), split_axis=0, concat_axis=0, tiled=T...]
    pallas_call x0 -> x1, Pallas kernels: none -> 33.9 us  [swap(): pl.pallas_call(functools.partial(swap_kernel, doms, grps), out_shape=jax....]
    pallas_call x1, Pallas kernels: 23.3 us -> 14.6 us  [deposit(): pl.pallas_call(functools.partial(deposit_kernel, capacity), out_shape=jax...]
    pallas_call x1, Pallas kernels: 55.8 us -> 54.2 us  [solve_grid(): pl.pallas_call(functools.partial(grid_kernel, doms, grps), out_shape=(jax...]
where the time goes in v3:
time: 115 us
  Pallas kernels  103 us (90%)
  local copies, waits for them, and re-layouts  5.43 us (5%)
  other arithmetic  5.12 us (4%)
  between operations  1.67 us (1%)
    pallas_call x1, Pallas kernels, solve_grid(): pl.pallas_call(functools.partial(grid_kernel, doms, grps), out_shape=(jax...  54.2 us
    pallas_call x1, Pallas kernels, swap(): pl.pallas_call(functools.partial(swap_kernel, doms, grps), out_shape=jax....  33.9 us
    pallas_call x1, Pallas kernels, deposit(): pl.pallas_call(functools.partial(deposit_kernel, capacity), out_shape=jax...  14.6 us

profile of v3, /device:TPU:0, one launch (start us, length us, event | category | flops | bytes accessed | tf_op | source)
XLA Modules:
  0.0 115.0 jit_solution(16402260257135688521)
XLA Ops:
  0.6 0.7 iota_compare_fusion.3
  1.4 0.7 add_convert_fusion
  2.1 0.7 fusion.7
  2.8 0.6 reduce-window.6
  3.4 0.2 slice_reduce_fusion
  3.6 0.8 fusion.6
  4.4 0.7 compare_select_fusion
  5.1 0.1 broadcast_and_fusion
  5.2 0.1 copy.27
  5.3 1.2 %scatter_custom_fusion.1 = f32[512,3]{1,0:T(8,128)S(1)} fusion(s32[256]{0:T(256)S(1)} %bitcast.39, f32[256,3]{1,0:T(8,128)S(1)} %copy.27, f32[]{:T(128)} %constant.23.clone.1), kind=kCustom, calls=%fused_computation.8 | custom fusion | bytes 6148 | tf_op jit(solution)/shard_map/scatter | solution.py:573
  6.5 0.2 copy.29
  6.8 0.2 copy.25
  7.0 0.1 bitcast_select_fusion
  7.1 0.2 copy.26
  7.3 1.7 %scatter_custom_fusion = f32[512,512]{1,0:T(8,128)S(1)} fusion(s32[256]{0:T(256)S(1)} %bitcast.40, f32[256,512]{1,0:T(8,128)S(1)} %copy.26, f32[]{:T(128)} %constant.23.clone.1), kind=kCustom, calls=%fused_computation.4 | custom fusion | bytes 1048580 | tf_op jit(solution)/shard_map/scatter | solution.py:572
  9.1 0.1 select_maximum_fusion.send_ref
  9.2 33.9 %swap.1.tiles_ref = f32[32,72,128]{2,1,0:T(8,128)S(1)} custom-call(f32[32,72,128]{2,1,0:T(8,128)S(1)} %select_maximum_fusion.send_ref), custom_call_target="tpu_custom_call" | custom-call | tf_op jit(solution)/shard_map/swap/pallas_call | solution.py:91
  43.3 0.1 convert_element_type.25.offsets_ref
  43.4 14.6 %deposit.1.deposit_ref = f32[16,64,128]{2,1,0:T(8,128)S(1)} custom-call(s32[1536]{0:T(1024)S(1)} %convert_element_type.25.offsets_ref, f32[32,72,128]{2,1,0:T(8,128)S(1)} %swap.1.tiles_ref), custom_call_target="tpu_custom_call" | custom-call | tf_op jit(solution)/shard_map/deposit/pallas_call | solution.py:151
  58.1 54.2 %grid.1 = (f32[8,64,128]{2,1,0:T(8,128)S(1)}, f32[8,128]{1,0:T(8,128)S(1)}) custom-call(f32[16,64,128]{2,1,0:T(8,128)S(1)} %deposit.1.deposit_ref, f32[8,64,128]{2,1,0:T(8,128)S(1)} %copy-done, f32[8,64,128]{2,1,0:T(8,128)S(1)} %copy-done.1, f32[128,128]{1,0:T(8,128)S(1)} %copy-done.8, f32[32,64]{1,0:T(8,128)S(1)} %copy-done.13, f32[128,128]{1,0:T(8,128)S(1)} %copy-done.7, ...), custom_call_target="tpu_custom_call" | custom-call | tf_op jit(solution)/shard_map/grid/pallas_call | solution.py:522
  112.4 0.1 slice_reduce_fusion.1
  112.5 0.6 slice.23
  113.8 0.5 multiply_subtract_fusion
  114.3 0.7 copy.36
  (40 shorter events, 0.3 us)
Async XLA Ops:
  0.6 6.2 %copy-start.15 = (f32[256,512]{1,0:T(8,128)S(1)}, f32[256,512]{1,0:T(8,128)}, u32[]{:S(2)}) copy-start(f32[256,512]{1,0:T(8,128)} %param.24) | copy-start | bytes 1572868
  43.1 14.9 %copy-start = (f32[8,64,128]{2,1,0:T(8,128)S(1)}, f32[8,64,128]{2,1,0:T(8,128)}, u32[]{:S(2)}) copy-start(f32[8,64,128]{2,1,0:T(8,128)} %valence_ref.1) | copy-start | bytes 786436
  43.1 14.9 %copy-start.1 = (f32[8,64,128]{2,1,0:T(8,128)S(1)}, f32[8,64,128]{2,1,0:T(8,128)}, u32[]{:S(2)}) copy-start(f32[8,64,128]{2,1,0:T(8,128)} %start_ref.1) | copy-start | bytes 786436
  43.1 14.9 %copy-start.2 = (f32[256,64]{1,0:T(8,128)S(1)}, f32[256,64]{1,0:T(8,128)}, u32[]{:S(2)}) copy-start(f32[256,64]{1,0:T(8,128)} %constant.61.clone.from_xy) | copy-start | bytes 196612
  43.1 14.9 %copy-start.3 = (f32[128,128]{1,0:T(8,128)S(1)}, f32[128,128]{1,0:T(8,128)}, u32[]{:S(2)}) copy-start(f32[128,128]{1,0:T(8,128)} %constant.65.clone.pz1) | copy-start | bytes 196612
  43.1 14.9 %copy-start.4 = (f32[128,128]{1,0:T(8,128)S(1)}, f32[128,128]{1,0:T(8,128)}, u32[]{:S(2)}) copy-start(f32[128,128]{1,0:T(8,128)} %constant.63.clone.pz2) | copy-start | bytes 196612
  43.1 14.9 %copy-start.5 = (f32[128,64]{1,0:T(8,128)S(1)}, f32[128,64]{1,0:T(8,128)}, u32[]{:S(2)}) copy-start(f32[128,64]{1,0:T(8,128)} %constant.59.clone.into_z) | copy-start | bytes 98308
  43.1 14.9 %copy-start.6 = (f32[64,256]{1,0:T(8,128)S(1)}, f32[64,256]{1,0:T(8,128)}, u32[]{:S(2)}) copy-start(f32[64,256]{1,0:T(8,128)} %constant.58.clone.into_xy) | copy-start | bytes 196612
  43.1 14.9 %copy-start.7 = (f32[128,128]{1,0:T(8,128)S(1)}, f32[128,128]{1,0:T(8,128)}, u32[]{:S(2)}) copy-start(f32[128,128]{1,0:T(8,128)} %constant.56.clone.rz2) | copy-start | bytes 196612
  43.2 14.9 %copy-start.8 = (f32[128,128]{1,0:T(8,128)S(1)}, f32[128,128]{1,0:T(8,128)}, u32[]{:S(2)}) copy-start(f32[128,128]{1,0:T(8,128)} %constant.54.clone.rz1) | copy-start | bytes 196612
  43.2 14.9 %copy-start.9 = (f32[64,32]{1,0:T(8,128)S(1)}, f32[64,32]{1,0:T(8,128)}, u32[]{:S(2)}) copy-start(f32[64,32]{1,0:T(8,128)} %constant.66.clone.py1) | copy-start | bytes 24580
  43.2 14.9 %copy-start.10 = (f32[64,128]{1,0:T(8,128)S(1)}, f32[64,128]{1,0:T(8,128)}, u32[]{:S(2)}) copy-start(f32[64,128]{1,0:T(8,128)} %constant.62.clone.from_z) | copy-start | bytes 98308
  43.2 14.9 %copy-start.11 = (f32[64,64]{1,0:T(8,128)S(1)}, f32[64,64]{1,0:T(8,128)}, u32[]{:S(2)}) copy-start(f32[64,64]{1,0:T(8,128)} %constant.60.clone.inverse) | copy-start | bytes 49156
  43.2 14.9 %copy-start.12 = (f32[32,16]{1,0:T(8,128)S(1)}, f32[32,16]{1,0:T(8,128)}, u32[]{:S(2)}) copy-start(f32[32,16]{1,0:T(8,128)} %constant.64.clone.py2) | copy-start | bytes 6148
  43.2 14.9 %copy-start.13 = (f32[32,64]{1,0:T(8,128)S(1)}, f32[32,64]{1,0:T(8,128)}, u32[]{:S(2)}) copy-start(f32[32,64]{1,0:T(8,128)} %constant.55.clone.ry1) | copy-start | bytes 24580
  43.2 14.9 %copy-start.14 = (f32[16,32]{1,0:T(8,128)S(1)}, f32[16,32]{1,0:T(8,128)}, u32[]{:S(2)}) copy-start(f32[16,32]{1,0:T(8,128)} %constant.57.clone.ry2) | copy-start | bytes 6148
  58.1 55.6 %copy-start.16 = (f32[6]{0:T(128)S(1)}, f32[6]{0:T(128)}, u32[]{:S(2)}) copy-start(f32[6]{0:T(128)} %constant.67.clone) | copy-start | bytes 76

commit v4 on v3

--- a/solution.py
+++ b/solution.py
@@ -262,15 +262,29 @@
 
     def exchange(src, planes, packed, faces_to, sides_to, send_sem, recv_sem):
         copies = [
-            send(packed, sides_to.at[k], send_sem.at[k], recv_sem.at[k], at(*CORNERS[k]))
+            (send(packed, sides_to.at[k], send_sem.at[k], recv_sem.at[k], at(*CORNERS[k])), CORNERS[k])
             for k in range(6)
         ]
         for k, (first, dx) in enumerate(((planes - h, 1), (0, -1))):
             part = src.at[pl.ds(first, h)]
-            copies.append(send(part, faces_to.at[k], send_sem.at[6 + k], recv_sem.at[6 + k], at(dx, 0)))
-        for copy in copies:
-            copy.start()
+            copy = send(part, faces_to.at[k], send_sem.at[6 + k], recv_sem.at[6 + k], at(dx, 0))
+            copies.append((copy, (dx, 0)))
+        copies = copies[6:] + copies[:6]
+        begin(copies)
         return copies
+
+    def exists(dx, dz):
+        x, z = dom + dx, grp + dz
+        return (x >= 0) & (x < doms) & (z >= 0) & (z < grps)
+
+    def begin(copies):
+        for copy, (dx, dz) in copies:
+            pl.when(exists(dx, dz))(copy.start)
+
+    def finish(copies):
+        for copy, (dx, dz) in copies:
+            pl.when(exists(-dx, -dz))(copy.wait_recv)
+            pl.when(exists(dx, dz))(copy.wait_send)
 
     def all_send_to(buf, which):
         def one(k):
@@ -305,24 +319,30 @@
         return ((x >= 0) & (x < doms * count)).astype(jnp.float32)
 
     def pack0(src, which):
-        total = jnp.zeros((ny, cz), jnp.float32)
+        total = jnp.zeros((ny // 2, cz), jnp.float32)
         for x in range(cx):
             kept = jnp.where(edge_lane, src[x], 0.0)
-            total = total + (kept if x == 0 else pltpu.roll(kept, 16 * x, 1))
+            top, bottom = kept[: ny // 2], kept[ny // 2 :]
+            total = total + (top if x == 0 else pltpu.roll(top, 8 * x, 1))
+            total = total + pltpu.roll(bottom, (8 * x + half) % cz, 1)
         edge[which] = total
 
     def widen0(src, which, dst):
-        from_up = lane % 16 < 8
+        from_up = lane % 8 < 4
         kinds = ((3, 2, 0, cx - h, 0), (1, 0, None, 0, h), (5, 4, 1, 0, cx + h))
         for up, down, face, first, place in kinds:
             mixed = jnp.where(from_up, sides[which, up], sides[which, down])
             for i in range(cx if face is None else h):
                 x = first + i
                 own = src[x] if face is None else faces[which, face, i]
-                far = mixed if x == 0 else pltpu.roll(mixed, cz - 16 * x, 1)
+                top = mixed if x == 0 else pltpu.roll(mixed, cz - 8 * x, 1)
+                bottom = pltpu.roll(mixed, (cz + half - 8 * x) % cz, 1)
+                far = jnp.concatenate([top, bottom], axis=0)
                 mask = inside(place + i, cx)
-                dst[place + i, :, 0:cz] = own * mask
-                dst[place + i, :, cz : 2 * cz] = far * (beside * mask)
+                if face is not None:
+                    own = jnp.where(mask * jnp.ones((1, cz), jnp.float32) > 0.0, own, 0.0)
+                dst[place + i, :, 0:cz] = own
+                dst[place + i, :, cz : 2 * cz] = jnp.where(beside * mask > 0.0, far, 0.0)
 
     def around(u, p, axis_y, axis_z):
         c = u[p]
@@ -331,32 +351,39 @@
         return c, total + pltpu.roll(c, 1, 1) + pltpu.roll(c, axis_z - 1, 1)
 
     def sweep0(src, dst, first, last):
-        def one(p, carry):
-            c, near = around(src, p, ny, 2 * cz)
-            new = c * (1.0 / 3.0) + (fe[p] + near) * (1.0 / 9.0)
-            dst[p] = new * (lanes0 * inside(p, cx))
+        def one(i, carry):
+            found = []
+            for p in (first + 2 * i, first + 2 * i + 1):
+                c, near = around(src, p, ny, 2 * cz)
+                new = c * (1.0 / 3.0) + (fe[p] + near) * (1.0 / 9.0)
+                found.append((p, new * (lanes0 * inside(p, cx))))
+            for p, new in found:
+                dst[p] = new
             return carry
 
-        lax.fori_loop(first, last, one, 0)
-
+        lax.fori_loop(0, (last - first) // 2, one, 0)
+
+    reach = cx - 1
+    copy = send(
+        deposit_ref.at[pl.ds(cx, reach)], spill, spill_sem.at[0], spill_sem.at[1], at(1, 0)
+    )
+    spilling = [(copy, (1, 0))]
+    begin(spilling)
     pack0(start_ref, 0)
     going_u = exchange(start_ref, cx, edge.at[0], faces.at[0], sides.at[0], ex_send.at[0], ex_recv.at[0])
-    spilling = send(
-        deposit_ref.at[pl.ds(cx, cx)], spill, spill_sem.at[0], spill_sem.at[1], at(1, 0)
-    )
-    spilling.start()
-    spilling.wait()
-    inner = (dom > 0).astype(jnp.float32)
+    finish(spilling)
+    has_spill = (dom > 0).astype(jnp.float32) * jnp.ones((1, cz), jnp.float32) > 0.0
     for x in range(cx):
-        second[0, x] = valence_ref[x] + (deposit_ref[x] + spill[x] * inner)
+        charge = deposit_ref[x]
+        if x < reach:
+            charge = charge + jnp.where(has_spill, spill[x], 0.0)
+        second[0, x] = valence_ref[x] + charge
     density = second.at[0]
     pack0(density, 1)
     going_f = exchange(density, cx, edge.at[1], faces.at[1], sides.at[1], ex_send.at[1], ex_recv.at[1])
-    for copy in going_u:
-        copy.wait()
+    finish(going_u)
     widen0(start_ref, 0, ua)
-    for copy in going_f:
-        copy.wait()
+    finish(going_f)
     widen0(density, 1, fe)
 
     sweep0(ua, ub, 1, cx + 2 * h - 1)
@@ -378,8 +405,7 @@
         kept = jnp.where(edge_lane1, f1[x], 0.0)
         total = total + (kept if x == 0 else pltpu.roll(kept, 8 * x, 1))
     edge1[...] = total
-    for copy in exchange(f1, c1, edge1, faces1, sides1, ex1_send, ex1_recv):
-        copy.wait()
+    finish(exchange(f1, c1, edge1, faces1, sides1, ex1_send, ex1_recv))
     from_up = lane < 40
     for up, down, face, first, place in ((3, 2, 0, c1 - h, 0), (1, 0, None, 0, h), (5, 4, 1, 0, c1 + h)):
         mixed = jnp.where(from_up, sides1[up], sides1[down])
@@ -387,7 +413,8 @@
             x = first + i
             own = f1[x] if face is None else faces1[face, i]
             far = pltpu.roll(mixed, half - 8 * x, 1)
-            value = jnp.where(lane < half, own, far) * (lanes1 * inside(place + i, c1))
+            mask = lanes1 * inside(place + i, c1)
+            value = jnp.where(mask > 0.0, jnp.where(lane < half, own, far), 0.0)
             ge[place + i] = value
             va[place + i] = value * (4.0 / 9.0)
 
@@ -470,8 +497,7 @@
             second[1, x] = ua[h + x, :, 0:cz] + fine
     update = second.at[1]
     pack0(update, 2)
-    for copy in exchange(update, cx, edge.at[2], faces.at[2], sides.at[2], ex_send.at[2], ex_recv.at[2]):
-        copy.wait()
+    finish(exchange(update, cx, edge.at[2], faces.at[2], sides.at[2], ex_send.at[2], ex_recv.at[2]))
     widen0(update, 2, ua)
     sweep0(ua, ub, 1, cx + 2 * h - 1)
     sweep0(ub, ua, 2, cx + 2 * h - 2)
@@ -528,8 +554,8 @@
         in_specs=[vmem] * (3 + len(constants)),
         out_specs=(vmem, vmem),
         scratch_shapes=[
-            wide, wide, wide, buf(cx, ny, cz), buf(2, cx, ny, cz),
-            buf(3, ny, cz), buf(3, 2, h, ny, cz), buf(3, 6, ny, cz),
+            wide, wide, wide, buf(cx - 1, ny, cz), buf(2, cx, ny, cz),
+            buf(3, ny // 2, cz), buf(3, 2, h, ny, cz), buf(3, 6, ny // 2, cz),
             buf(c1, y1, cz), buf(y1, cz), buf(2, h, y1, cz), buf(6, y1, cz),
             wide1, wide1, wide1,
             buf(2 * doms, y2, z2), whole, whole, buf(n, 8, cz), buf(n, 8, cz),

time: 115 us -> 106 us (0.922)
  Pallas kernels: 103 us -> 93.1 us
    pallas_call x1, Pallas kernels: 54.2 us -> 44.6 us  [solve_grid(): pl.pallas_call(functools.partial(grid_kernel, doms, grps), out_shape=(jax...]
where the time goes in v4:
time: 106 us; the launch traced here: 105 us
  Pallas kernels  93.1 us (88%)
  local copies, waits for them, and re-layouts  5.43 us (5%)
  other arithmetic  5.12 us (5%)
  between operations  1.67 us (2%)
    pallas_call x1, Pallas kernels, solve_grid(): pl.pallas_call(functools.partial(grid_kernel, doms, grps), out_shape=(jax...  44.6 us
    pallas_call x1, Pallas kernels, swap(): pl.pallas_call(functools.partial(swap_kernel, doms, grps), out_shape=jax....  33.9 us
    pallas_call x1, Pallas kernels, deposit(): pl.pallas_call(functools.partial(deposit_kernel, capacity), out_shape=jax...  14.6 us

profile of v4, /device:TPU:0, one launch (start us, length us, event | category | flops | bytes accessed | tf_op | source)
XLA Modules:
  0.0 105.3 jit_solution(1611919741006307154)
XLA Ops:
  0.6 0.7 iota_compare_fusion.3
  1.4 0.7 add_convert_fusion
  2.1 0.7 fusion.7
  2.8 0.6 reduce-window.6
  3.4 0.2 slice_reduce_fusion
  3.6 0.8 fusion.6
  4.4 0.7 compare_select_fusion
  5.1 0.1 broadcast_and_fusion
  5.2 0.1 copy.27
  5.3 1.2 %scatter_custom_fusion.1 = f32[512,3]{1,0:T(8,128)S(1)} fusion(s32[256]{0:T(256)S(1)} %bitcast.39, f32[256,3]{1,0:T(8,128)S(1)} %copy.27, f32[]{:T(128)} %constant.23.clone.1), kind=kCustom, calls=%fused_computation.8 | custom fusion | bytes 6148 | tf_op jit(solution)/shard_map/scatter | solution.py:599
  6.5 0.2 copy.29
  6.8 0.2 copy.25
  7.0 0.1 bitcast_select_fusion
  7.1 0.2 copy.26
  7.3 1.7 %scatter_custom_fusion = f32[512,512]{1,0:T(8,128)S(1)} fusion(s32[256]{0:T(256)S(1)} %bitcast.40, f32[256,512]{1,0:T(8,128)S(1)} %copy.26, f32[]{:T(128)} %constant.23.clone.1), kind=kCustom, calls=%fused_computation.4 | custom fusion | bytes 1048580 | tf_op jit(solution)/shard_map/scatter | solution.py:598
  9.1 0.1 select_maximum_fusion.send_ref
  9.2 33.9 %swap.1.tiles_ref = f32[32,72,128]{2,1,0:T(8,128)S(1)} custom-call(f32[32,72,128]{2,1,0:T(8,128)S(1)} %select_maximum_fusion.send_ref), custom_call_target="tpu_custom_call" | custom-call | tf_op jit(solution)/shard_map/swap/pallas_call | solution.py:91
  43.3 0.1 convert_element_type.25.offsets_ref
  43.4 14.6 %deposit.1.deposit_ref = f32[16,64,128]{2,1,0:T(8,128)S(1)} custom-call(s32[1536]{0:T(1024)S(1)} %convert_element_type.25.offsets_ref, f32[32,72,128]{2,1,0:T(8,128)S(1)} %swap.1.tiles_ref), custom_call_target="tpu_custom_call" | custom-call | tf_op jit(solution)/shard_map/deposit/pallas_call | solution.py:151
  58.1 44.6 %grid.1 = (f32[8,64,128]{2,1,0:T(8,128)S(1)}, f32[8,128]{1,0:T(8,128)S(1)}) custom-call(f32[16,64,128]{2,1,0:T(8,128)S(1)} %deposit.1.deposit_ref, f32[8,64,128]{2,1,0:T(8,128)S(1)} %copy-done, f32[8,64,128]{2,1,0:T(8,128)S(1)} %copy-done.1, f32[128,128]{1,0:T(8,128)S(1)} %copy-done.8, f32[32,64]{1,0:T(8,128)S(1)} %copy-done.13, f32[128,128]{1,0:T(8,128)S(1)} %copy-done.7, ...), custom_call_target="tpu_custom_call" | custom-call | tf_op jit(solution)/shard_map/grid/pallas_call | solution.py:548
  102.8 0.1 slice_reduce_fusion.1
  102.9 0.6 slice.23
  104.1 0.5 multiply_subtract_fusion
  104.6 0.7 copy.36
  (40 shorter events, 0.3 us)
Async XLA Ops:
  0.6 6.2 %copy-start.15 = (f32[256,512]{1,0:T(8,128)S(1)}, f32[256,512]{1,0:T(8,128)}, u32[]{:S(2)}) copy-start(f32[256,512]{1,0:T(8,128)} %param.24) | copy-start | bytes 1572868
  43.1 14.9 %copy-start = (f32[8,64,128]{2,1,0:T(8,128)S(1)}, f32[8,64,128]{2,1,0:T(8,128)}, u32[]{:S(2)}) copy-start(f32[8,64,128]{2,1,0:T(8,128)} %valence_ref.1) | copy-start | bytes 786436
  43.1 14.9 %copy-start.1 = (f32[8,64,128]{2,1,0:T(8,128)S(1)}, f32[8,64,128]{2,1,0:T(8,128)}, u32[]{:S(2)}) copy-start(f32[8,64,128]{2,1,0:T(8,128)} %start_ref.1) | copy-start | bytes 786436
  43.1 14.9 %copy-start.2 = (f32[256,64]{1,0:T(8,128)S(1)}, f32[256,64]{1,0:T(8,128)}, u32[]{:S(2)}) copy-start(f32[256,64]{1,0:T(8,128)} %constant.61.clone.from_xy) | copy-start | bytes 196612
  43.1 14.9 %copy-start.3 = (f32[128,128]{1,0:T(8,128)S(1)}, f32[128,128]{1,0:T(8,128)}, u32[]{:S(2)}) copy-start(f32[128,128]{1,0:T(8,128)} %constant.65.clone.pz1) | copy-start | bytes 196612
  43.1 14.9 %copy-start.4 = (f32[128,128]{1,0:T(8,128)S(1)}, f32[128,128]{1,0:T(8,128)}, u32[]{:S(2)}) copy-start(f32[128,128]{1,0:T(8,128)} %constant.63.clone.pz2) | copy-start | bytes 196612
  43.1 14.9 %copy-start.5 = (f32[128,64]{1,0:T(8,128)S(1)}, f32[128,64]{1,0:T(8,128)}, u32[]{:S(2)}) copy-start(f32[128,64]{1,0:T(8,128)} %constant.59.clone.into_z) | copy-start | bytes 98308
  43.1 14.9 %copy-start.6 = (f32[64,256]{1,0:T(8,128)S(1)}, f32[64,256]{1,0:T(8,128)}, u32[]{:S(2)}) copy-start(f32[64,256]{1,0:T(8,128)} %constant.58.clone.into_xy) | copy-start | bytes 196612
  43.1 14.9 %copy-start.7 = (f32[128,128]{1,0:T(8,128)S(1)}, f32[128,128]{1,0:T(8,128)}, u32[]{:S(2)}) copy-start(f32[128,128]{1,0:T(8,128)} %constant.56.clone.rz2) | copy-start | bytes 196612
  43.2 14.9 %copy-start.8 = (f32[128,128]{1,0:T(8,128)S(1)}, f32[128,128]{1,0:T(8,128)}, u32[]{:S(2)}) copy-start(f32[128,128]{1,0:T(8,128)} %constant.54.clone.rz1) | copy-start | bytes 196612
  43.2 14.9 %copy-start.9 = (f32[64,32]{1,0:T(8,128)S(1)}, f32[64,32]{1,0:T(8,128)}, u32[]{:S(2)}) copy-start(f32[64,32]{1,0:T(8,128)} %constant.66.clone.py1) | copy-start | bytes 24580
  43.2 14.9 %copy-start.10 = (f32[64,128]{1,0:T(8,128)S(1)}, f32[64,128]{1,0:T(8,128)}, u32[]{:S(2)}) copy-start(f32[64,128]{1,0:T(8,128)} %constant.62.clone.from_z) | copy-start | bytes 98308
  43.2 14.9 %copy-start.11 = (f32[64,64]{1,0:T(8,128)S(1)}, f32[64,64]{1,0:T(8,128)}, u32[]{:S(2)}) copy-start(f32[64,64]{1,0:T(8,128)} %constant.60.clone.inverse) | copy-start | bytes 49156
  43.2 14.9 %copy-start.12 = (f32[32,16]{1,0:T(8,128)S(1)}, f32[32,16]{1,0:T(8,128)}, u32[]{:S(2)}) copy-start(f32[32,16]{1,0:T(8,128)} %constant.64.clone.py2) | copy-start | bytes 6148
  43.2 14.9 %copy-start.13 = (f32[32,64]{1,0:T(8,128)S(1)}, f32[32,64]{1,0:T(8,128)}, u32[]{:S(2)}) copy-start(f32[32,64]{1,0:T(8,128)} %constant.55.clone.ry1) | copy-start | bytes 24580
  43.2 14.9 %copy-start.14 = (f32[16,32]{1,0:T(8,128)S(1)}, f32[16,32]{1,0:T(8,128)}, u32[]{:S(2)}) copy-start(f32[16,32]{1,0:T(8,128)} %constant.57.clone.ry2) | copy-start | bytes 6148
  58.1 46.0 %copy-start.16 = (f32[6]{0:T(128)S(1)}, f32[6]{0:T(128)}, u32[]{:S(2)}) copy-start(f32[6]{0:T(128)} %constant.67.clone) | copy-start | bytes 76

commit v5 on v4

--- a/solution.py
+++ b/solution.py
@@ -47,7 +47,40 @@
     return [out[:, width * i : width * i + width] for i in range(count)]
 
 
-def swap_kernel(doms, grps, send_ref, got_ref, send_sem, recv_sem):
+def pack_tiles(n, capacity, info_ref, tiles_ref, send_ref):
+    atoms = tiles_ref.shape[0]
+    slots = n * capacity
+    info = info_ref[...]
+    home, size = info[:, 3:4], info[:, 4:5]
+    named = lax.broadcasted_iota(jnp.int32, (atoms, n), 1) == home
+    named = jnp.where(named, 1.0, 0.0)
+    earlier = lax.broadcasted_iota(jnp.int32, (atoms, atoms), 1)
+    earlier = earlier < lax.broadcasted_iota(jnp.int32, (atoms, atoms), 0)
+    earlier = jnp.where(earlier, 1.0, 0.0).astype(jnp.bfloat16)
+    before = jnp.dot(earlier, named.astype(jnp.bfloat16), preferred_element_type=jnp.float32)
+    rank = jnp.sum(before * named, axis=1, keepdims=True).astype(jnp.int32)
+    slot = home * capacity + rank
+    place = lax.broadcasted_iota(jnp.int32, (atoms, slots), 1) == slot
+    place = jnp.where(place, 1.0, 0.0).astype(jnp.bfloat16)
+    first_dims = (((0,), (0,)), ((), ()))
+    lane = lax.broadcasted_iota(jnp.int32, (1, 128), 1)
+    for q in range(4):
+        largest = jnp.maximum(2 * q + lane // 64, jnp.maximum((lane // 8) % 8, lane % 8))
+        kept = jnp.where(largest < size, tiles_ref[:, 128 * q : 128 * q + 128], 0.0)
+        stacked = jnp.concatenate(parts_of(kept), axis=1)
+        out = lax.dot_general(place, stacked, first_dims, preferred_element_type=jnp.float32)
+        out = out[:, 0:128] + (out[:, 128:256] + out[:, 256:384])
+        send_ref[:, capacity * q : capacity * q + capacity, :] = out.reshape(n, capacity, 128)
+    numbers = info.astype(jnp.float32).astype(jnp.bfloat16)
+    rows = lax.dot_general(numbers, place, first_dims, preferred_element_type=jnp.float32)
+    for d in range(n):
+        tile, shift = divmod(d * capacity, 128)
+        part = rows[:, 128 * tile : 128 * tile + 128]
+        part = part if shift == 0 else pltpu.roll(part, 128 - shift, 1)
+        send_ref[d, 4 * capacity : 4 * capacity + OFFSET_ROWS, :] = part
+
+
+def swap_kernel(doms, grps, capacity, info_ref, tiles_ref, got_ref, send_ref, send_sem, recv_sem):
     n = doms * grps
     me = lax.axis_index("dom") * grps + lax.axis_index("grp")
 
@@ -78,27 +111,30 @@
         return carry
 
     lax.fori_loop(1, n, greet, 0)
+    pack_tiles(n, capacity, info_ref, tiles_ref, send_ref)
     pl.semaphore_wait(barrier, n - 1)
     lax.fori_loop(1, n, go, 0)
     got_ref[me] = send_ref[me]
     lax.fori_loop(1, n, done, 0)
 
 
-def swap(send):
+def swap(info, tiles, capacity):
     doms, grps = lax.axis_size("dom"), lax.axis_size("grp")
+    n = doms * grps
     vmem = pl.BlockSpec(memory_space=pltpu.VMEM)
     dma = pltpu.SemaphoreType.DMA
+    shape = (n, 4 * capacity + OFFSET_ROWS, 128)
     return pl.pallas_call(
-        functools.partial(swap_kernel, doms, grps),
-        out_shape=jax.ShapeDtypeStruct(send.shape, jnp.float32),
-        in_specs=[vmem],
+        functools.partial(swap_kernel, doms, grps, capacity),
+        out_shape=jax.ShapeDtypeStruct(shape, jnp.float32),
+        in_specs=[vmem, vmem],
         out_specs=vmem,
-        scratch_shapes=[dma((doms * grps,)), dma((doms * grps,))],
+        scratch_shapes=[pltpu.VMEM(shape, jnp.float32), dma((n,)), dma((n,))],
         compiler_params=pltpu.CompilerParams(
             collective_id=1, has_side_effects=True, vmem_limit_bytes=32 * 1024 * 1024
         ),
         name="swap",
-    )(send)
+    )(info, tiles)
 
 
 def deposit_kernel(capacity, offsets_ref, tiles_ref, out_ref, *grids):
@@ -113,13 +149,13 @@
         for j, grid in enumerate(grids):
             slot = i * len(grids) + j
             device = slot // capacity
-            first = (slot % capacity) * 4
+            first = slot % capacity
             at_x = offsets_ref[slot]
             at_y = width_y + TE - offsets_ref[slots + slot]
             at_z = offsets_ref[2 * slots + slot]
             parts = []
             for q in range(4):
-                line = tiles_ref[device, pl.ds(first + q, 1), :]
+                line = tiles_ref[device, pl.ds(q * capacity + first, 1), :]
                 line = jnp.broadcast_to(line, (TE, 128))
                 line = pltpu.roll(line, 0, 1, stride=TE, stride_axis=0)
                 for mask, shift in ((low, (at_z + 72) % 128), (high, (at_z + 8) % 128)):
@@ -584,24 +620,10 @@
     atoms_here = atom_tiles.shape[0]
     tile_cells = atom_tiles.shape[1]
     capacity = 2 * atoms_here // device_count
-    tile_index = jnp.arange(TE, dtype=jnp.int32)
-    inside = tile_index[None, :] < atom_size
-    inside_cube = inside[:, :, None, None] & inside[:, None, :, None] & inside[:, None, None, :]
-    masked = atom_tiles * inside_cube.reshape(atom_tiles.shape).astype(jnp.float32)
-    targets = jnp.arange(device_count, dtype=jnp.int32)
-    matches = (atom_home == targets[None, :]).astype(jnp.int32)
-    before = jnp.cumsum(matches, axis=0) - matches
-    slot_rank = jnp.sum(before * matches, axis=1)
-    slot_index = atom_home[:, 0] * capacity + slot_rank
-    offsets = jnp.concatenate([atom_offset_x, atom_offset_y, atom_offset_z], axis=1)
-    slots = device_count * capacity
-    send_tiles = jnp.zeros((slots, tile_cells), jnp.float32).at[slot_index].set(masked)
-    send_offsets = jnp.zeros((slots, 3), jnp.float32).at[slot_index].set(offsets.astype(jnp.float32))
-    send_offsets = send_offsets.reshape(device_count, capacity, 3).transpose(0, 2, 1)
-    send_offsets = jnp.pad(send_offsets, ((0, 0), (0, OFFSET_ROWS - 3), (0, 128 - capacity)))
+    info = jnp.concatenate([atom_offset_x, atom_offset_y, atom_offset_z, atom_home, atom_size], axis=1)
+    info = jnp.pad(info, ((0, 0), (0, OFFSET_ROWS - info.shape[1])))
     tile_rows = capacity * tile_cells // 128
-    send = jnp.concatenate([send_tiles.reshape(device_count, tile_rows, 128), send_offsets], axis=1)
-    got = swap(send)
+    got = swap(info, atom_tiles, capacity)
     got_offsets = got[:, tile_rows : tile_rows + 3, :capacity].transpose(1, 0, 2)
     got_offsets = got_offsets.reshape(-1).astype(jnp.int32)
     width_x, width_y, width_z = valence.shape

time: 106 us -> 98.8 us (0.932)
  other arithmetic: 5.12 us -> 0.64 us
  local copies, waits for them, and re-layouts: 5.43 us -> 3.43 us
    scatter x2 -> x0, local copies, waits for them, and re-layouts: 2.9 us -> none  [the longest x1 1.68 us: shards(): jnp.zeros((slots, tile_cells), jnp.float32).at[slot_index].set(masked)]
    convert_element_type x2 -> x0, other arithmetic: 1.41 us -> none  [the longest x1 0.72 us: shards(): offsets.astype(jnp.float32)]
where the time goes in v5:
time: 98.8 us; the launch traced here: 98.6 us
  Pallas kernels  92.9 us (94%)
  local copies, waits for them, and re-layouts  3.43 us (3%)
  between operations  1.6 us (2%)
    pallas_call x1, Pallas kernels, solve_grid(): pl.pallas_call(functools.partial(grid_kernel, doms, grps), out_shape=(jax...  44.7 us
    pallas_call x1, Pallas kernels, swap(): pl.pallas_call(functools.partial(swap_kernel, doms, grps, capacity), out_...  33.6 us
    pallas_call x1, Pallas kernels, deposit(): pl.pallas_call(functools.partial(deposit_kernel, capacity), out_shape=jax...  14.6 us

profile of v5, /device:TPU:0, one launch (start us, length us, event | category | flops | bytes accessed | tf_op | source)
XLA Modules:
  0.0 98.6 jit_solution(302984341865664639)
XLA Ops:
  0.6 0.8 concatenate.3
  1.4 0.1 copy.35
  1.6 1.0 %copy-done = f32[256,512]{1,0:T(8,128)S(1)} copy-done((f32[256,512]{1,0:T(8,128)S(1)}, f32[256,512]{1,0:T(8,128)}, u32[]{:S(2)}) %copy-start) | copy-done | bytes 524312
  2.6 33.6 %swap.1.tiles_ref = f32[32,72,128]{2,1,0:T(8,128)S(1)} custom-call(s32[256,8]{1,0:T(8,128)S(1)} %pad.4.info_ref, f32[256,512]{1,0:T(8,128)S(1)} %copy-done), custom_call_target="tpu_custom_call" | custom-call | tf_op jit(solution)/shard_map/swap/pallas_call | solution.py:127
  36.2 0.0 copy-start.3
  36.3 0.0 copy-start.4
  36.3 0.0 copy-start.5
  36.3 0.0 copy-start.6
  36.3 0.0 copy-start.7
  36.3 0.0 copy-start.8
  36.3 0.0 copy-start.9
  36.3 0.0 copy-start.10
  36.4 0.0 copy-start.12
  36.4 0.0 copy-start.13
  36.4 0.0 copy-start.14
  36.4 0.0 copy-start.15
  36.4 0.1 convert_element_type.9.offsets_ref
  36.5 14.6 %deposit.1.deposit_ref = f32[16,64,128]{2,1,0:T(8,128)S(1)} custom-call(s32[1536]{0:T(1024)S(1)} %convert_element_type.9.offsets_ref, f32[32,72,128]{2,1,0:T(8,128)S(1)} %swap.1.tiles_ref), custom_call_target="tpu_custom_call" | custom-call | tf_op jit(solution)/shard_map/deposit/pallas_call | solution.py:187
  51.3 0.0 copy-start.16
  51.3 44.7 %grid.1 = (f32[8,64,128]{2,1,0:T(8,128)S(1)}, f32[8,128]{1,0:T(8,128)S(1)}) custom-call(f32[16,64,128]{2,1,0:T(8,128)S(1)} %deposit.1.deposit_ref, f32[8,64,128]{2,1,0:T(8,128)S(1)} %copy-done.1, f32[8,64,128]{2,1,0:T(8,128)S(1)} %copy-done.2, f32[128,128]{1,0:T(8,128)S(1)} %copy-done.9, f32[32,64]{1,0:T(8,128)S(1)} %copy-done.14, f32[128,128]{1,0:T(8,128)S(1)} %copy-done.8, ...), custom_call_target="tpu_custom_call" | custom-call | tf_op jit(solution)/shard_map/grid/pallas_call | solution.py:584
  96.0 0.1 slice_reduce_fusion
  96.1 0.6 slice.15
  97.4 0.5 multiply_subtract_fusion
  97.9 0.7 copy.38
  (23 shorter events, 0.1 us)
Async XLA Ops:
  1.6 1.0 %copy-start = (f32[256,512]{1,0:T(8,128)S(1)}, f32[256,512]{1,0:T(8,128)}, u32[]{:S(2)}) copy-start(f32[256,512]{1,0:T(8,128)} %tiles_ref.1) | copy-start | bytes 1572868
  36.2 14.9 %copy-start.1 = (f32[8,64,128]{2,1,0:T(8,128)S(1)}, f32[8,64,128]{2,1,0:T(8,128)}, u32[]{:S(2)}) copy-start(f32[8,64,128]{2,1,0:T(8,128)} %valence_ref.1) | copy-start | bytes 786436
  36.2 14.9 %copy-start.2 = (f32[8,64,128]{2,1,0:T(8,128)S(1)}, f32[8,64,128]{2,1,0:T(8,128)}, u32[]{:S(2)}) copy-start(f32[8,64,128]{2,1,0:T(8,128)} %start_ref.1) | copy-start | bytes 786436
  36.2 14.9 %copy-start.3 = (f32[256,64]{1,0:T(8,128)S(1)}, f32[256,64]{1,0:T(8,128)}, u32[]{:S(2)}) copy-start(f32[256,64]{1,0:T(8,128)} %constant.48.clone.from_xy) | copy-start | bytes 196612
  36.3 14.9 %copy-start.4 = (f32[128,128]{1,0:T(8,128)S(1)}, f32[128,128]{1,0:T(8,128)}, u32[]{:S(2)}) copy-start(f32[128,128]{1,0:T(8,128)} %constant.52.clone.pz1) | copy-start | bytes 196612
  36.3 14.9 %copy-start.5 = (f32[128,128]{1,0:T(8,128)S(1)}, f32[128,128]{1,0:T(8,128)}, u32[]{:S(2)}) copy-start(f32[128,128]{1,0:T(8,128)} %constant.50.clone.pz2) | copy-start | bytes 196612
  36.3 14.9 %copy-start.6 = (f32[128,64]{1,0:T(8,128)S(1)}, f32[128,64]{1,0:T(8,128)}, u32[]{:S(2)}) copy-start(f32[128,64]{1,0:T(8,128)} %constant.46.clone.into_z) | copy-start | bytes 98308
  36.3 14.9 %copy-start.7 = (f32[64,256]{1,0:T(8,128)S(1)}, f32[64,256]{1,0:T(8,128)}, u32[]{:S(2)}) copy-start(f32[64,256]{1,0:T(8,128)} %constant.45.clone.into_xy) | copy-start | bytes 196612
  36.3 14.9 %copy-start.8 = (f32[128,128]{1,0:T(8,128)S(1)}, f32[128,128]{1,0:T(8,128)}, u32[]{:S(2)}) copy-start(f32[128,128]{1,0:T(8,128)} %constant.43.clone.rz2) | copy-start | bytes 196612
  36.3 14.9 %copy-start.9 = (f32[128,128]{1,0:T(8,128)S(1)}, f32[128,128]{1,0:T(8,128)}, u32[]{:S(2)}) copy-start(f32[128,128]{1,0:T(8,128)} %constant.41.clone.rz1) | copy-start | bytes 196612
  36.3 14.9 %copy-start.10 = (f32[64,32]{1,0:T(8,128)S(1)}, f32[64,32]{1,0:T(8,128)}, u32[]{:S(2)}) copy-start(f32[64,32]{1,0:T(8,128)} %constant.53.clone.py1) | copy-start | bytes 24580
  36.3 14.9 %copy-start.11 = (f32[64,128]{1,0:T(8,128)S(1)}, f32[64,128]{1,0:T(8,128)}, u32[]{:S(2)}) copy-start(f32[64,128]{1,0:T(8,128)} %constant.49.clone.from_z) | copy-start | bytes 98308
  36.4 14.9 %copy-start.12 = (f32[64,64]{1,0:T(8,128)S(1)}, f32[64,64]{1,0:T(8,128)}, u32[]{:S(2)}) copy-start(f32[64,64]{1,0:T(8,128)} %constant.47.clone.inverse) | copy-start | bytes 49156
  36.4 14.9 %copy-start.13 = (f32[32,16]{1,0:T(8,128)S(1)}, f32[32,16]{1,0:T(8,128)}, u32[]{:S(2)}) copy-start(f32[32,16]{1,0:T(8,128)} %constant.51.clone.py2) | copy-start | bytes 6148
  36.4 14.9 %copy-start.14 = (f32[32,64]{1,0:T(8,128)S(1)}, f32[32,64]{1,0:T(8,128)}, u32[]{:S(2)}) copy-start(f32[32,64]{1,0:T(8,128)} %constant.42.clone.ry1) | copy-start | bytes 24580
  36.4 14.9 %copy-start.15 = (f32[16,32]{1,0:T(8,128)S(1)}, f32[16,32]{1,0:T(8,128)}, u32[]{:S(2)}) copy-start(f32[16,32]{1,0:T(8,128)} %constant.44.clone.ry2) | copy-start | bytes 6148
  51.3 46.1 %copy-start.16 = (f32[6]{0:T(128)S(1)}, f32[6]{0:T(128)}, u32[]{:S(2)}) copy-start(f32[6]{0:T(128)} %constant.54.clone) | copy-start | bytes 76

commit v6 on v5

--- a/solution.py
+++ b/solution.py
@@ -387,17 +387,16 @@
         return c, total + pltpu.roll(c, 1, 1) + pltpu.roll(c, axis_z - 1, 1)
 
     def sweep0(src, dst, first, last):
+        count = (last - first) // 2
+
         def one(i, carry):
-            found = []
-            for p in (first + 2 * i, first + 2 * i + 1):
+            for p in [first + count * i + k for k in range(count)]:
                 c, near = around(src, p, ny, 2 * cz)
                 new = c * (1.0 / 3.0) + (fe[p] + near) * (1.0 / 9.0)
-                found.append((p, new * (lanes0 * inside(p, cx))))
-            for p, new in found:
-                dst[p] = new
+                dst[p] = new * (lanes0 * inside(p, cx))
             return carry
 
-        lax.fori_loop(0, (last - first) // 2, one, 0)
+        lax.fori_loop(0, 2, one, 0)
 
     reach = cx - 1
     copy = send(

time: 98.8 us -> 97.7 us (0.989)
  Pallas kernels: 92.9 us -> 91.9 us
    pallas_call x1, Pallas kernels: 44.7 us -> 43.7 us  [solve_grid(): pl.pallas_call(functools.partial(grid_kernel, doms, grps), out_shape=(jax...]
where the time goes in v6:
time: 97.7 us; the launch traced here: 97.6 us
  Pallas kernels  91.9 us (94%)
  local copies, waits for them, and re-layouts  3.43 us (4%)
  between operations  1.6 us (2%)
    pallas_call x1, Pallas kernels, solve_grid(): pl.pallas_call(functools.partial(grid_kernel, doms, grps), out_shape=(jax...  43.7 us
    pallas_call x1, Pallas kernels, swap(): pl.pallas_call(functools.partial(swap_kernel, doms, grps, capacity), out_...  33.6 us
    pallas_call x1, Pallas kernels, deposit(): pl.pallas_call(functools.partial(deposit_kernel, capacity), out_shape=jax...  14.6 us

profile of v6, /device:TPU:0, one launch (start us, length us, event | category | flops | bytes accessed | tf_op | source)
XLA Modules:
  0.0 97.6 jit_solution(17095341904581385865)
XLA Ops:
  0.6 0.8 concatenate.3
  1.4 0.1 copy.35
  1.6 1.0 %copy-done = f32[256,512]{1,0:T(8,128)S(1)} copy-done((f32[256,512]{1,0:T(8,128)S(1)}, f32[256,512]{1,0:T(8,128)}, u32[]{:S(2)}) %copy-start) | copy-done | bytes 524312
  2.6 33.6 %swap.1.tiles_ref = f32[32,72,128]{2,1,0:T(8,128)S(1)} custom-call(s32[256,8]{1,0:T(8,128)S(1)} %pad.4.info_ref, f32[256,512]{1,0:T(8,128)S(1)} %copy-done), custom_call_target="tpu_custom_call" | custom-call | tf_op jit(solution)/shard_map/swap/pallas_call | solution.py:127
  36.2 0.0 copy-start.3
  36.3 0.0 copy-start.4
  36.3 0.0 copy-start.5
  36.3 0.0 copy-start.6
  36.3 0.0 copy-start.7
  36.3 0.0 copy-start.8
  36.3 0.0 copy-start.9
  36.3 0.0 copy-start.10
  36.4 0.0 copy-start.12
  36.4 0.0 copy-start.13
  36.4 0.0 copy-start.14
  36.4 0.0 copy-start.15
  36.4 0.1 convert_element_type.9.offsets_ref
  36.5 14.6 %deposit.1.deposit_ref = f32[16,64,128]{2,1,0:T(8,128)S(1)} custom-call(s32[1536]{0:T(1024)S(1)} %convert_element_type.9.offsets_ref, f32[32,72,128]{2,1,0:T(8,128)S(1)} %swap.1.tiles_ref), custom_call_target="tpu_custom_call" | custom-call | tf_op jit(solution)/shard_map/deposit/pallas_call | solution.py:187
  51.3 0.0 copy-start.16
  51.3 43.7 %grid.1 = (f32[8,64,128]{2,1,0:T(8,128)S(1)}, f32[8,128]{1,0:T(8,128)S(1)}) custom-call(f32[16,64,128]{2,1,0:T(8,128)S(1)} %deposit.1.deposit_ref, f32[8,64,128]{2,1,0:T(8,128)S(1)} %copy-done.1, f32[8,64,128]{2,1,0:T(8,128)S(1)} %copy-done.2, f32[128,128]{1,0:T(8,128)S(1)} %copy-done.9, f32[32,64]{1,0:T(8,128)S(1)} %copy-done.14, f32[128,128]{1,0:T(8,128)S(1)} %copy-done.8, ...), custom_call_target="tpu_custom_call" | custom-call | tf_op jit(solution)/shard_map/grid/pallas_call | solution.py:583
  95.0 0.1 slice_reduce_fusion
  95.1 0.6 slice.15
  96.3 0.5 multiply_subtract_fusion
  96.8 0.7 copy.38
  (23 shorter events, 0.1 us)
Async XLA Ops:
  1.6 1.0 %copy-start = (f32[256,512]{1,0:T(8,128)S(1)}, f32[256,512]{1,0:T(8,128)}, u32[]{:S(2)}) copy-start(f32[256,512]{1,0:T(8,128)} %tiles_ref.1) | copy-start | bytes 1572868
  36.2 14.9 %copy-start.1 = (f32[8,64,128]{2,1,0:T(8,128)S(1)}, f32[8,64,128]{2,1,0:T(8,128)}, u32[]{:S(2)}) copy-start(f32[8,64,128]{2,1,0:T(8,128)} %valence_ref.1) | copy-start | bytes 786436
  36.2 14.9 %copy-start.2 = (f32[8,64,128]{2,1,0:T(8,128)S(1)}, f32[8,64,128]{2,1,0:T(8,128)}, u32[]{:S(2)}) copy-start(f32[8,64,128]{2,1,0:T(8,128)} %start_ref.1) | copy-start | bytes 786436
  36.2 14.9 %copy-start.3 = (f32[256,64]{1,0:T(8,128)S(1)}, f32[256,64]{1,0:T(8,128)}, u32[]{:S(2)}) copy-start(f32[256,64]{1,0:T(8,128)} %constant.48.clone.from_xy) | copy-start | bytes 196612
  36.3 14.9 %copy-start.4 = (f32[128,128]{1,0:T(8,128)S(1)}, f32[128,128]{1,0:T(8,128)}, u32[]{:S(2)}) copy-start(f32[128,128]{1,0:T(8,128)} %constant.52.clone.pz1) | copy-start | bytes 196612
  36.3 14.9 %copy-start.5 = (f32[128,128]{1,0:T(8,128)S(1)}, f32[128,128]{1,0:T(8,128)}, u32[]{:S(2)}) copy-start(f32[128,128]{1,0:T(8,128)} %constant.50.clone.pz2) | copy-start | bytes 196612
  36.3 14.9 %copy-start.6 = (f32[128,64]{1,0:T(8,128)S(1)}, f32[128,64]{1,0:T(8,128)}, u32[]{:S(2)}) copy-start(f32[128,64]{1,0:T(8,128)} %constant.46.clone.into_z) | copy-start | bytes 98308
  36.3 14.9 %copy-start.7 = (f32[64,256]{1,0:T(8,128)S(1)}, f32[64,256]{1,0:T(8,128)}, u32[]{:S(2)}) copy-start(f32[64,256]{1,0:T(8,128)} %constant.45.clone.into_xy) | copy-start | bytes 196612
  36.3 14.9 %copy-start.8 = (f32[128,128]{1,0:T(8,128)S(1)}, f32[128,128]{1,0:T(8,128)}, u32[]{:S(2)}) copy-start(f32[128,128]{1,0:T(8,128)} %constant.43.clone.rz2) | copy-start | bytes 196612
  36.3 14.9 %copy-start.9 = (f32[128,128]{1,0:T(8,128)S(1)}, f32[128,128]{1,0:T(8,128)}, u32[]{:S(2)}) copy-start(f32[128,128]{1,0:T(8,128)} %constant.41.clone.rz1) | copy-start | bytes 196612
  36.3 14.9 %copy-start.10 = (f32[64,32]{1,0:T(8,128)S(1)}, f32[64,32]{1,0:T(8,128)}, u32[]{:S(2)}) copy-start(f32[64,32]{1,0:T(8,128)} %constant.53.clone.py1) | copy-start | bytes 24580
  36.3 14.9 %copy-start.11 = (f32[64,128]{1,0:T(8,128)S(1)}, f32[64,128]{1,0:T(8,128)}, u32[]{:S(2)}) copy-start(f32[64,128]{1,0:T(8,128)} %constant.49.clone.from_z) | copy-start | bytes 98308
  36.4 14.9 %copy-start.12 = (f32[64,64]{1,0:T(8,128)S(1)}, f32[64,64]{1,0:T(8,128)}, u32[]{:S(2)}) copy-start(f32[64,64]{1,0:T(8,128)} %constant.47.clone.inverse) | copy-start | bytes 49156
  36.4 14.9 %copy-start.13 = (f32[32,16]{1,0:T(8,128)S(1)}, f32[32,16]{1,0:T(8,128)}, u32[]{:S(2)}) copy-start(f32[32,16]{1,0:T(8,128)} %constant.51.clone.py2) | copy-start | bytes 6148
  36.4 14.9 %copy-start.14 = (f32[32,64]{1,0:T(8,128)S(1)}, f32[32,64]{1,0:T(8,128)}, u32[]{:S(2)}) copy-start(f32[32,64]{1,0:T(8,128)} %constant.42.clone.ry1) | copy-start | bytes 24580
  36.4 14.9 %copy-start.15 = (f32[16,32]{1,0:T(8,128)S(1)}, f32[16,32]{1,0:T(8,128)}, u32[]{:S(2)}) copy-start(f32[16,32]{1,0:T(8,128)} %constant.44.clone.ry2) | copy-start | bytes 6148
  51.3 45.0 %copy-start.16 = (f32[6]{0:T(128)S(1)}, f32[6]{0:T(128)}, u32[]{:S(2)}) copy-start(f32[6]{0:T(128)} %constant.54.clone) | copy-start | bytes 76
